TPU v7x, 256 devices: a whole 4x4x8 slice. The times are simulated.
256 devices in a mesh: seq: 128 (over y_lo, x, z, core), tp: 2 (over y_hi).
Axes of the slice: x: 4, y: 4 (y_hi: 2, y_lo: 2; y = y_hi * 2 + y_lo), z: 8, core: 2. Of those that a mesh axis runs over, the one named last changes fastest.
Arguments:
- response_query: bfloat16 [128, 512, 5120], P('seq', None, 'tp')
- response_kv: bfloat16 [128, 512, 2, 1024], P('seq', None, None, 'tp'), may hold values from -6 to 6
- prompt_cache: bfloat16 [128, 16, 2, 1024], P('seq', 'tp')
- prompt_order: int32 [16], replicated, may hold values from 0 to 15, each once
- response_prompt: int32 [128], P('seq'), may hold values from 0 to 15
- response_length: int32 [128], P('seq'), may hold values from 1 to 512, 32768 in all
- out_grad: bfloat16 [128, 512, 5120], P('seq', None, 'tp'), may hold values from -6 to 6
Outputs:
- attention_out: bfloat16 [128, 512, 5120], P('seq', None, 'tp')
- query_grad: bfloat16 [128, 512, 5120], P('seq', None, 'tp')
- response_kv_grad: bfloat16 [128, 512, 2, 1024], P('seq', None, None, 'tp')
- prompt_cache_grad: bfloat16 [128, 16, 2, 1024], P('seq', 'tp')
Inputs may be any that keep to these rules, and one draw needn't show every extreme that they name: prompt_order names each of the 16 prompts once. `response_length`: some response has all 512 tokens live.
All inputs are finite; a program needn't handle non-finite values. No bound on the sum of `response_length` on one device may be relied on, other than what follows from the above.
Results may differ from a plain program's by a relative error of at most 0.0065.
Values may be sent and summed in bfloat16 or wider, within the bound.
A program may use at most 128 MiB of HBM per device.

v0:
```python
import math

import jax
import jax.numpy as jnp
from jax import lax
from jax.sharding import PartitionSpec as P

HQ = 40
KVH = 8
HD = 128
PLEN = 128
RMAX = 512


def head_step(query, key_rows, value_rows, grad_live, length):
    total_rows = query.shape[0]
    width = key_rows.shape[0]
    scale = 1.0 / math.sqrt(HD)
    position = lax.broadcasted_iota(jnp.int32, (total_rows, width), 0)
    column = lax.broadcasted_iota(jnp.int32, (total_rows, width), 1)
    offset = column - PLEN
    allowed = (column < PLEN) | (offset <= position) & (offset < length)
    live_rows = lax.broadcasted_iota(jnp.int32, (total_rows, 1), 0) < length
    scores = jnp.einsum("tgd,ld->gtl", query, key_rows, preferred_element_type=jnp.float32) * scale
    scores = jnp.where(allowed, scores, -1e30)
    highest = jnp.max(scores, axis=-1, keepdims=True)
    raised = jnp.exp(scores - highest)
    probs = raised / jnp.sum(raised, axis=-1, keepdims=True) * live_rows.astype(jnp.float32)
    probs_low = probs.astype(jnp.bfloat16)
    result = jnp.einsum(
        "gtl,ld->tgd", probs_low, value_rows, preferred_element_type=jnp.float32
    ).astype(jnp.bfloat16)
    dprobs = jnp.einsum("tgd,ld->gtl", grad_live, value_rows, preferred_element_type=jnp.float32)
    center = jnp.sum(probs * dprobs, axis=-1, keepdims=True)
    dscores = (probs * (dprobs - center)).astype(jnp.bfloat16)
    query_grad = (
        jnp.einsum("gtl,ld->tgd", dscores, key_rows, preferred_element_type=jnp.float32) * scale
    ).astype(jnp.bfloat16)
    key_grad = jnp.einsum("gtl,tgd->ld", dscores, query, preferred_element_type=jnp.float32) * scale
    value_grad = jnp.einsum("gtl,tgd->ld", probs_low, grad_live, preferred_element_type=jnp.float32)
    return (result, query_grad, key_grad, value_grad)


def block_table(owners, prompt_order):
    return (owners[:, None] == prompt_order[None, :]).astype(jnp.float32)


def block_index(owners, prompt_order):
    blocks = jnp.arange(prompt_order.shape[0], dtype=jnp.int32)
    return jnp.sum(jnp.where(owners[:, None] == prompt_order[None, :], blocks[None, :], 0), axis=1)


def local(
    response_query,
    response_kv,
    prompt_cache,
    prompt_order,
    response_prompt,
    response_length,
    out_grad,
):
    width = response_kv.shape[3]
    local_heads = width // HD
    group = HQ // KVH
    span = PLEN + RMAX
    halves = lax.all_to_all(prompt_cache, "tp", split_axis=3, concat_axis=1, tiled=True)
    everything = lax.all_gather(halves, "seq", axis=0, tiled=True)
    prefixes = jnp.take(everything, block_index(response_prompt, prompt_order), axis=1)
    prefixes = prefixes.transpose(1, 0, 2, 3)

    def visit(carry, items):
        query, own_rows, grad, length, prefix = items
        key_rows = (
            jnp.concatenate([prefix[:, 0], own_rows[:, 0]], 0)
            .reshape(span, local_heads, HD)
            .transpose(1, 0, 2)
        )
        value_rows = (
            jnp.concatenate([prefix[:, 1], own_rows[:, 1]], 0)
            .reshape(span, local_heads, HD)
            .transpose(1, 0, 2)
        )
        live_rows = lax.broadcasted_iota(jnp.int32, (RMAX, 1), 0) < length
        grad_live = jnp.where(live_rows, grad, jnp.zeros_like(grad))
        shaped = query.reshape(RMAX, local_heads, group, HD).transpose(1, 0, 2, 3)
        grad_shaped = grad_live.reshape(RMAX, local_heads, group, HD).transpose(1, 0, 2, 3)

        def per_head(parts):
            return head_step(parts[0], parts[1], parts[2], parts[3], length)

        result, query_grad, key_grad, value_grad = lax.map(
            per_head, (shaped, key_rows, value_rows, grad_shaped)
        )
        result = result.transpose(1, 0, 2, 3).reshape(RMAX, local_heads * group * HD)
        query_grad = query_grad.transpose(1, 0, 2, 3).reshape(RMAX, local_heads * group * HD)
        key_grad = key_grad.transpose(1, 0, 2).reshape(span, width)
        value_grad = value_grad.transpose(1, 0, 2).reshape(span, width)
        paired = jnp.stack([key_grad, value_grad], 1)
        return (carry, (result, query_grad, paired[PLEN:].astype(jnp.bfloat16), paired[:PLEN]))

    unused, outputs = lax.scan(
        visit,
        jnp.zeros((), jnp.float32),
        (response_query, response_kv, out_grad, response_length, prefixes),
    )
    attention_out, query_grad, response_kv_grad, prefix_terms = outputs
    terms = prefix_terms.transpose(1, 0, 2, 3)
    dense = jnp.einsum(
        "lrcw,rp->lpcw",
        terms,
        block_table(response_prompt, prompt_order),
        precision=lax.Precision.HIGHEST,
    )
    summed = lax.psum_scatter(dense, "seq", scatter_dimension=0, tiled=True)
    rounded = summed.astype(jnp.bfloat16)
    prompt_cache_grad = lax.all_to_all(rounded, "tp", split_axis=1, concat_axis=3, tiled=True)
    return (attention_out, query_grad, response_kv_grad, prompt_cache_grad)


def solution(mesh):
    return jax.shard_map(
        local,
        mesh=mesh,
        in_specs=(
            P("seq", None, "tp"),
            P("seq", None, None, "tp"),
            P("seq", "tp", None, None),
            P(),
            P("seq"),
            P("seq"),
            P("seq", None, "tp"),
        ),
        out_specs=(
            P("seq", None, "tp"),
            P("seq", None, "tp"),
            P("seq", None, None, "tp"),
            P("seq", "tp", None, None),
        ),
        check_vma=False,
    )
```

profile of v0, /device:TPU:1, one launch (start us, length us, event | category | flops | bytes accessed | tf_op | source)
XLA Modules:
  0.0 938.8 jit_solution(16060671713726951905)
XLA Ops:
  7.2 1.3 copy.83
  9.0 9.1 all_to_all.36
  18.1 0.6 reshape.135
  19.1 0.6 copy.117
  20.5 1.3 fusion.85
  23.8 2.5 copy.88
  26.2 3.0 copy.91
  29.9 4.4 copy.90
  34.8 2.1 fusion.95
  36.9 1.7 select_bitcast_fusion
  38.6 198.4 %all-gather.2.cloned.1.call-done = bf16[128,16,2,512]{3,1,2,0:T(8,128)(2,1)} async-done(((bf16[1,16,2,512]{3,1,2,0:T(8,128)(2,1)}), bf16[128,16,2,512]{3,1,2,0:T(8,128)(2,1)}) %all-gather.2.cloned.1.call-update) | async-done | bytes 4194320 | tf_op jit(solution)/shard_map/all_gather | solution.py:67
  237.0 2.1 constant_dynamic-slice_fusion
  239.6 1.0 maximum_bitcast_fusion
  240.6 95.6 %while.32 = (s32[]{:T(128)}, bf16[4,512,5,128]{1,3,2,0:T(8,128)(2,1)}, bf16[4,512,5,128]{1,3,2,0:T(8,128)(2,1)}, f32[4,640,128]{2,1,0:T(8,128)}, f32[4,640,128]{...) while((s32[]{:T(128)}, ...), condition=%wide.region_5.6_spmd, body=%wide.region_1.5_spmd.sunk | while | flops 2549761536 | bytes 83994304 | solution.py:91
  240.6 0.7 iota_compare_fusion.5
  241.6 6.5 fusion.129
  248.1 0.6 fusion.130
  248.7 4.3 fusion.132
  253.1 0.6 slice-done.1
  253.7 1.9 fusion.133
  255.6 1.5 fusion.134
  257.1 2.8 fusion.135
  260.0 2.9 fusion.136
  262.8 1.7 fusion.131
  264.5 0.7 iota_compare_fusion.5
  265.5 6.5 fusion.129
  272.0 0.6 fusion.130
  272.7 4.3 fusion.132
  277.6 1.9 fusion.133
  279.5 1.5 fusion.134
  281.1 2.8 fusion.135
  283.9 2.9 fusion.136
  286.7 1.7 fusion.131
  288.4 0.7 iota_compare_fusion.5
  289.4 6.5 fusion.129
  295.9 0.6 fusion.130
  296.6 4.3 fusion.132
  300.9 0.6 slice-done.1
  301.5 1.9 fusion.133
  303.4 1.5 fusion.134
  304.9 2.8 fusion.135
  307.8 2.9 fusion.136
  310.6 1.7 fusion.131
  312.3 0.7 iota_compare_fusion.5
  313.3 6.5 fusion.129
  319.8 0.6 fusion.130
  320.5 4.3 fusion.132
  324.8 0.6 slice-done.1
  325.4 1.9 fusion.133
  327.3 1.5 fusion.134
  328.9 2.8 fusion.135
  331.7 2.8 fusion.136
  334.5 1.7 fusion.131
  336.2 2.3 copy.95
  338.5 0.8 copy.96
  339.8 4.5 multiply_bitcast_fusion
  344.3 570.3 %reduce-scatter.2.cloned.1.call-done = f32[1,16,2,512]{3,1,2,0:T(8,128)} async-done(((f32[128,16,2,512]{3,1,2,0:T(8,128)}), f32[1,16,2,512]{3,1,2,0:T(8,128)}) %reduce-scatter.2.cloned.1.call-update) | async-done | bytes 65552 | tf_op jit(solution)/shard_map/reduce_scatter | solution.py:114
  914.6 0.8 convert_element_type.48
  915.5 0.6 copy.97
  916.1 3.7 all-to-all-start.1
  919.8 2.7 fusion.83
  922.5 4.4 copy.100
  926.9 4.4 copy.99
  931.3 0.6 copy.101
  (62 shorter events, 4.4 us)
Async XLA Ops:
  7.2 16.6 %copy-start.2 = (bf16[1,512,2,512]{3,2,1,0:T(2,128)(2,1)S(1)}, bf16[1,512,2,512]{3,2,1,0:T(2,128)(2,1)}, u32[]{:S(2)}) copy-start(bf16[1,512,2,512]{3,2,1,0:T(2,128)(2,1)} %param.10) | copy-start | bytes 3145732
  7.2 229.9 %all-gather.2.cloned.1.call-start = ((), (), s32[]{:S(2)}) async-start(), calls=%async_computation.3 | async-start | bytes 4227072 | tf_op jit(solution)/shard_map/all_gather | solution.py:67
  19.8 894.9 %reduce-scatter.2.cloned.1.call-start = ((), (), s32[]{:S(2)}) async-start(), calls=%async_computation.4 | async-start | bytes 8454144 | tf_op jit(solution)/shard_map/reduce_scatter | solution.py:114
  29.9 4.4 copy-start.5
  38.6 201.0 %copy-start = (bf16[512,1,512]{0,2,1:T(8,128)(2,1)S(1)}, bf16[512,1,512]{0,2,1:T(8,128)(2,1)}, u32[]{:S(2)}) copy-start(bf16[512,1,512]{0,2,1:T(8,128)(2,1)} %get-tuple-element.260) | copy-start | bytes 1572868
  241.6 7.1 copy-start.3
  248.7 4.4 slice-start
  248.7 5.0 slice-start.1
  265.5 7.1 copy-start.3
  272.6 4.4 slice-start
  272.6 5.0 slice-start.1
  289.4 7.1 copy-start.3
  296.5 4.4 slice-start
  296.5 5.0 slice-start.1
  313.3 7.1 copy-start.3
  320.4 4.4 slice-start
  320.5 5.0 slice-start.1
  336.2 2.3 copy-start.1
  338.5 1.3 copy-start.4
  916.1 15.2 %all-to-all-start.1 = ((bf16[1,16,2,512]{3,2,0,1:T(2,128)(2,1)}), bf16[1,16,2,512]{3,2,0,1:T(2,128)(2,1)S(1)}, u32[]{:S(2)}, u32[]{:S(2)}) async-start(bf16[1,16,2,512]{3,2,0,1:T(2,128)(2,1)} %copy.97), calls=%async_computation.2 | async-start | bytes 65536 | tf_op jit(solution)/shard_map/all_to_all | solution.py:116
Sparse Core Ops, SparseCore 0:
  19.9 217.0 all-gather.1
  344.4 570.1 reduce-scatter.1
where the time goes:
time: 946 us; the launch traced here: 939 us
  waiting for transfers between devices  769 us (81%)
  matrix products  78.7 us (8%)
  local copies, waits for them, and re-layouts  33.4 us (4%)
  other arithmetic  27.2 us (3%)
  between operations  17.5 us (2%)
    reduce_scatter x1, waiting for transfers between devices, local(): summed = lax.psum_scatter(dense, 'seq', scatter_dimension=0, tiled=True)  570 us
    all_gather x1, waiting for transfers between devices, local(): everything = lax.all_gather(halves, 'seq', axis=0, tiled=True)  198 us
    sub x4, matrix products, head_step(): raised = jnp.exp(scores - highest)  25.8 us
    unnamed x19, local copies, waits for them, and re-layouts  21.7 us
  transfers between devices with their start and end apart: 3, of which 2 were waited for; matrix products, arithmetic and copies ran while one was open for 3% of the time, Pallas kernels for 0%

commit v1 on v0

v1 whole, which is shorter than its diff:
```python
import functools
import math

import jax
import jax.numpy as jnp
from jax import lax
from jax.experimental import pallas as pl
from jax.experimental.pallas import tpu as pltpu
from jax.sharding import PartitionSpec as P

HQ = 40
KVH = 8
HD = 128
PLEN = 128
RMAX = 512
GROUP = HQ // KVH
ROWS = 128
TILES = RMAX // ROWS
STACK = GROUP * ROWS
STARTS = (0, 128, 384, 768)
WIDE = 1280
SCALE = 1.0 / math.sqrt(HD)
LOG2 = SCALE * math.log2(math.e)
F32 = jnp.float32
BF16 = jnp.bfloat16
MESH = pl.DeviceIdType.MESH


def dot_nn(a, b):
    return lax.dot_general(a, b, (((1,), (0,)), ((), ())), preferred_element_type=F32)


def dot_nt(a, b):
    return lax.dot_general(a, b, (((1,), (1,)), ((), ())), preferred_element_type=F32)


def dot_tn(a, b):
    return lax.dot_general(a, b, (((0,), (0,)), ((), ())), preferred_element_type=F32)


class Grid:
    def __init__(self, seq, tp, blocks):
        self.nb = 16 if seq >= 128 else 4
        self.na = seq // self.nb
        self.nt = tp
        self.nu = self.na * tp
        self.bl = blocks // tp
        self.c1 = self.bl * 2
        self.c2 = self.na * 2

    def here(self):
        seq, t = lax.axis_index("seq"), lax.axis_index("tp")
        a, b = seq // self.nb, lax.rem(seq, self.nb)
        return a, b, t, a * self.nt + t

    def plane(self, u, b):
        return {"seq": (u // self.nt) * self.nb + b, "tp": lax.rem(u, self.nt)}

    def column(self, a, b, t):
        return {"seq": a * self.nb + b, "tp": t}


def greet(grid):
    a, b, t, u = grid.here()
    barrier = pltpu.get_barrier_semaphore()

    def plane(o, carry):
        peer = lax.rem(u + o, grid.nu)
        pl.semaphore_signal(barrier, inc=1, device_id=grid.plane(peer, b), device_id_type=MESH)
        return carry

    def column(o, carry):
        peer = lax.rem(b + o, grid.nb)
        pl.semaphore_signal(barrier, inc=1, device_id=grid.column(a, peer, t), device_id_type=MESH)
        return carry

    lax.fori_loop(1, grid.nu, plane, 0)
    lax.fori_loop(1, grid.nb, column, 0)
    pl.semaphore_wait(barrier, grid.nu + grid.nb - 2)


def plane_copy(grid, o, source, target, send, recv):
    a, b, t, u = grid.here()
    peer = lax.rem(u + o, grid.nu)
    return pltpu.make_async_remote_copy(
        src_ref=source(peer),
        dst_ref=target(u),
        send_sem=send.at[o],
        recv_sem=recv.at[o],
        device_id=grid.plane(peer, b),
        device_id_type=MESH,
    )


def column_copy(grid, o, source, target, send, recv):
    a, b, t, u = grid.here()
    peer = lax.rem(b + o, grid.nb)
    return pltpu.make_async_remote_copy(
        src_ref=source(peer),
        dst_ref=target(b),
        send_sem=send.at[o],
        recv_sem=recv.at[o],
        device_id=grid.column(a, peer, t),
        device_id_type=MESH,
    )


def start_all(copy, count):
    def step(o, carry):
        copy(o).start()
        return carry

    lax.fori_loop(1, count, step, 0)


def wait_recv_all(copy, count):
    def step(o, carry):
        copy(o).wait_recv()
        return carry

    lax.fori_loop(1, count, step, 0)


def wait_send_all(copy, count):
    def step(o, carry):
        copy(o).wait_send()
        return carry

    lax.fori_loop(1, count, step, 0)


def chunk(ref, size):
    return lambda i: ref.at[pl.ds(pl.multiple_of(i * size, size), size)]


def choice(grid, picks):
    rows, cols = grid.nb * grid.c2, grid.nu * grid.c1
    row = lax.broadcasted_iota(jnp.int32, (rows, cols), 0)
    col = lax.broadcasted_iota(jnp.int32, (rows, cols), 1)
    inner = row % grid.c2
    kv, a = inner // grid.na, inner % grid.na
    wanted = a * (grid.nt * grid.c1) + picks.astype(jnp.int32) * 2 + kv
    return jnp.where(col == wanted, 1.0, 0.0).astype(BF16)


def shuffle(grid):
    rows = grid.nb * grid.c2
    row = lax.broadcasted_iota(jnp.int32, (rows, rows), 0)
    col = lax.broadcasted_iota(jnp.int32, (rows, rows), 1)
    half = grid.nb * grid.na
    kv, b, a = row // half, (row % half) // grid.na, row % grid.na
    return jnp.where(col == b * grid.c2 + kv * grid.na + a, 1.0, 0.0).astype(BF16)


def gather_kernel(
    grid,
    cache_ref,
    order_ref,
    owner_ref,
    rows_ref,
    pick_ref,
    mark,
    marks,
    first,
    chosen,
    second,
    send_m,
    recv_m,
    send_1,
    recv_1,
    send_2,
    recv_2,
):
    a, b, t, u = grid.here()
    greet(grid)
    first_copy = lambda o: plane_copy(
        grid, o, lambda peer: cache_ref.at[lax.rem(peer, grid.nt)], chunk(first, grid.c1), send_1, recv_1
    )
    start_all(first_copy, grid.nu)
    owner = owner_ref[0]
    block = jnp.int32(0)
    for i in range(order_ref.shape[0]):
        block = block + jnp.where(order_ref[i] == owner, i, 0)
    mark[...] = jnp.full(mark.shape, block.astype(F32), F32)
    mark_copy = lambda o: column_copy(grid, o, lambda peer: mark, chunk(marks, grid.c2), send_m, recv_m)
    start_all(mark_copy, grid.nb)
    first[pl.ds(pl.multiple_of(u * grid.c1, grid.c1), grid.c1)] = cache_ref[t]
    marks[pl.ds(pl.multiple_of(b * grid.c2, grid.c2), grid.c2)] = mark[...]
    wait_recv_all(mark_copy, grid.nb)
    wide = grid.nu * grid.c1 // marks.shape[1]
    pick = choice(grid, jnp.concatenate([marks[...]] * wide, 1) if wide > 1 else marks[:, : grid.nu * grid.c1])
    pick_ref[...] = pick
    wait_recv_all(first_copy, grid.nu)
    chosen[...] = dot_nn(pick, first[...]).astype(BF16)
    second_copy = lambda o: column_copy(grid, o, chunk(chosen, grid.c2), chunk(second, grid.c2), send_2, recv_2)
    start_all(second_copy, grid.nb)
    mine = pl.ds(pl.multiple_of(b * grid.c2, grid.c2), grid.c2)
    second[mine] = chosen[mine]
    wait_recv_all(second_copy, grid.nb)
    rows_ref[...] = dot_nn(shuffle(grid), second[...]).astype(BF16)
    wait_send_all(first_copy, grid.nu)
    wait_send_all(mark_copy, grid.nb)
    wait_send_all(second_copy, grid.nb)


def reduce_kernel(
    grid,
    terms_ref,
    pick_ref,
    out_ref,
    outgoing,
    third,
    dense,
    fourth,
    send_3,
    recv_3,
    send_4,
    recv_4,
):
    a, b, t, u = grid.here()
    outgoing[...] = dot_tn(shuffle(grid), terms_ref[...]).astype(BF16)
    greet(grid)
    third_copy = lambda o: column_copy(grid, o, chunk(outgoing, grid.c2), chunk(third, grid.c2), send_3, recv_3)
    start_all(third_copy, grid.nb)
    mine = pl.ds(pl.multiple_of(b * grid.c2, grid.c2), grid.c2)
    third[mine] = outgoing[mine]
    wait_recv_all(third_copy, grid.nb)
    dense[...] = dot_tn(pick_ref[...], third[...]).astype(BF16)
    fourth_copy = lambda o: plane_copy(grid, o, chunk(dense, grid.c1), chunk(fourth, grid.c1), send_4, recv_4)
    start_all(fourth_copy, grid.nu)
    own = pl.ds(pl.multiple_of(u * grid.c1, grid.c1), grid.c1)
    fourth[own] = dense[own]
    wait_recv_all(fourth_copy, grid.nu)
    for half in range(grid.nt):
        total = jnp.zeros((grid.c1, fourth.shape[1]), F32)
        for at in range(half, grid.nu, grid.nt):
            total = total + fourth[at * grid.c1 : (at + 1) * grid.c1].astype(F32)
        out_ref[half] = total.astype(BF16)
    wait_send_all(third_copy, grid.nb)
    wait_send_all(fourth_copy, grid.nu)


def attend_kernel(
    length_ref,
    q_ref,
    g_ref,
    k_ref,
    v_ref,
    rows_ref,
    out_ref,
    dq_ref,
    dk_ref,
    dv_ref,
    terms_ref,
    scores,
    dprobs,
    raised,
    front,
    center,
    inverse,
    scaled_q,
    scaled_g,
    sum_k,
    sum_v,
):
    heads = k_ref.shape[1] // HD
    length = length_ref[0]

    def stacked(ref, kv, i):
        return jnp.concatenate(
            [
                ref[i * ROWS : (i + 1) * ROWS, pl.ds(pl.multiple_of(kv * STACK + h * HD, HD), HD)]
                for h in range(GROUP)
            ],
            0,
        )

    def lanes(kv):
        return pl.ds(pl.multiple_of(kv * HD, HD), HD)

    def own_scores(kv, carry):
        for i in range(TILES):
            seen = (i + 1) * ROWS
            scores[:, STARTS[i] : STARTS[i] + seen] = dot_nt(stacked(q_ref, kv, i), k_ref[:seen, lanes(kv)])
            dprobs[:, STARTS[i] : STARTS[i] + seen] = dot_nt(stacked(g_ref, kv, i), v_ref[:seen, lanes(kv)])
        return carry

    tri = lax.broadcasted_iota(jnp.int32, (ROWS, ROWS), 1) <= lax.broadcasted_iota(jnp.int32, (ROWS, ROWS), 0)
    rows_at = lax.broadcasted_iota(jnp.int32, (ROWS, HD), 0)

    def prompt_part(kv, carry):
        front_k = rows_ref[:PLEN, lanes(kv)]
        front_v = rows_ref[PLEN:, lanes(kv)]
        term_k = jnp.zeros((PLEN, HD), F32)
        term_v = jnp.zeros((PLEN, HD), F32)
        for i in range(TILES):
            seen = (i + 1) * ROWS
            base = STARTS[i]
            query = stacked(q_ref, kv, i)
            grad = stacked(g_ref, kv, i)
            first = dot_nt(query, front_k)
            first_dp = dot_nt(grad, front_v)
            first_e = []
            for h in range(GROUP):
                part = slice(h * ROWS, (h + 1) * ROWS)
                f = first[part]
                own = [scores[part, base + j * ROWS : base + (j + 1) * ROWS] for j in range(i + 1)]
                own[i] = jnp.where(tri, own[i], -1e30)
                top = f
                for piece in own:
                    top = jnp.maximum(top, piece)
                top = jnp.max(top, axis=-1, keepdims=True)
                first_e.append(jnp.exp2((f - top) * LOG2).astype(BF16))
                for j in range(i + 1):
                    raised[part, base + j * ROWS : base + (j + 1) * ROWS] = jnp.exp2(
                        (own[j] - top) * LOG2
                    ).astype(BF16)
            first_e = jnp.concatenate(first_e, 0)
            both = jnp.concatenate([front_v, v_ref[:seen, lanes(kv)]], 0)
            both = jnp.concatenate([both, jnp.ones((PLEN + seen, HD), BF16)], 1)
            weights = jnp.concatenate([first_e, raised[:, base : base + seen]], 1)
            result = dot_nn(weights, both)
            live = rows_at + i * ROWS < length
            first_s, new_q, new_g = [], [], []
            for h in range(GROUP):
                part = slice(h * ROWS, (h + 1) * ROWS)
                inv = jnp.where(live, 1.0 / result[part, HD:], 0.0)
                value = result[part, :HD] * inv
                out_ref[i * ROWS : (i + 1) * ROWS, pl.ds(pl.multiple_of(kv * STACK + h * HD, HD), HD)] = value.astype(
                    BF16
                )
                gf = grad[part].astype(F32)
                mid = jnp.broadcast_to(jnp.sum(gf * value, axis=-1, keepdims=True), (ROWS, HD))
                center[i, part] = mid
                inverse[i, part] = inv * SCALE
                new_q.append((query[part].astype(F32) * (inv * SCALE)).astype(BF16))
                new_g.append((gf * inv).astype(BF16))
                first_s.append((first_e[part].astype(F32) * (first_dp[part] - mid)).astype(BF16))
            first_s = jnp.concatenate(first_s, 0)
            new_q = jnp.concatenate(new_q, 0)
            new_g = jnp.concatenate(new_g, 0)
            front[i] = first_s
            scaled_q[i] = new_q
            scaled_g[i] = new_g
            term_k = term_k + dot_tn(first_s, new_q)
            term_v = term_v + dot_tn(first_e, new_g)
        terms_ref[:PLEN, lanes(kv)] = term_k.astype(BF16)
        terms_ref[PLEN:, lanes(kv)] = term_v.astype(BF16)
        return carry

    def own_part(kv, carry):
        front_k = rows_ref[:PLEN, lanes(kv)]
        sum_k[...] = jnp.zeros_like(sum_k)
        sum_v[...] = jnp.zeros_like(sum_v)
        for i in range(TILES):
            seen = (i + 1) * ROWS
            base = STARTS[i]
            weights = raised[:, base : base + seen]
            own_s = []
            for j in range(i + 1):
                at = base + j * ROWS
                own_s.append(
                    jnp.concatenate(
                        [
                            (
                                raised[h * ROWS : (h + 1) * ROWS, at : at + ROWS].astype(F32)
                                * (
                                    dprobs[h * ROWS : (h + 1) * ROWS, at : at + ROWS]
                                    - center[i, h * ROWS : (h + 1) * ROWS]
                                )
                            ).astype(BF16)
                            for h in range(GROUP)
                        ],
                        0,
                    )
                )
            own_s = jnp.concatenate(own_s, 1)
            keys = jnp.concatenate([front_k, k_ref[:seen, lanes(kv)]], 0)
            grad_q = dot_nn(jnp.concatenate([front[i], own_s], 1), keys) * inverse[i]
            for h in range(GROUP):
                dq_ref[i * ROWS : (i + 1) * ROWS, pl.ds(pl.multiple_of(kv * STACK + h * HD, HD), HD)] = grad_q[
                    h * ROWS : (h + 1) * ROWS
                ].astype(BF16)
            sum_k[:seen] += dot_tn(own_s, scaled_q[i])
            sum_v[:seen] += dot_tn(weights, scaled_g[i])
        dk_ref[:, lanes(kv)] = sum_k[...].astype(BF16)
        dv_ref[:, lanes(kv)] = sum_v[...].astype(BF16)
        return carry

    def head(kv, carry):
        own_scores(kv, carry)
        prompt_part(kv, carry)
        own_part(kv, carry)
        return carry

    lax.fori_loop(0, heads, head, 0)


def attend(length, q, g, k, v, rows):
    heads = k.shape[1] // HD
    vmem = pl.BlockSpec(memory_space=pltpu.VMEM)
    stack = (TILES, STACK, HD)
    return pl.pallas_call(
        attend_kernel,
        out_shape=(
            jax.ShapeDtypeStruct(q.shape, BF16),
            jax.ShapeDtypeStruct(q.shape, BF16),
            jax.ShapeDtypeStruct(k.shape, BF16),
            jax.ShapeDtypeStruct(k.shape, BF16),
            jax.ShapeDtypeStruct(rows.shape, BF16),
        ),
        in_specs=[pl.BlockSpec(memory_space=pltpu.SMEM)] + [vmem] * 5,
        out_specs=(vmem,) * 5,
        scratch_shapes=[
            pltpu.VMEM((STACK, WIDE), F32),
            pltpu.VMEM((STACK, WIDE), F32),
            pltpu.VMEM((STACK, WIDE), BF16),
            pltpu.VMEM(stack, BF16),
            pltpu.VMEM(stack, F32),
            pltpu.VMEM(stack, F32),
            pltpu.VMEM(stack, BF16),
            pltpu.VMEM(stack, BF16),
            pltpu.VMEM((RMAX, HD), F32),
            pltpu.VMEM((RMAX, HD), F32),
        ],
        compiler_params=pltpu.CompilerParams(vmem_limit_bytes=63 * 1024 * 1024),
    )(length, q, g, k, v, rows)


def local(
    grid,
    response_query,
    response_kv,
    prompt_cache,
    prompt_order,
    response_prompt,
    response_length,
    out_grad,
):
    width = response_kv.shape[3]
    vmem = pl.BlockSpec(memory_space=pltpu.VMEM)
    smem = pl.BlockSpec(memory_space=pltpu.SMEM)
    dma = pltpu.SemaphoreType.DMA
    cache = prompt_cache.reshape(grid.c1, grid.nt, width).transpose(1, 0, 2)
    all_rows = grid.nb * grid.c2
    all_blocks = grid.nu * grid.c1
    rows, pick = pl.pallas_call(
        functools.partial(gather_kernel, grid),
        out_shape=(
            jax.ShapeDtypeStruct((all_rows, width), BF16),
            jax.ShapeDtypeStruct((all_rows, all_blocks), BF16),
        ),
        in_specs=[vmem, smem, smem],
        out_specs=(vmem, vmem),
        scratch_shapes=[
            pltpu.VMEM((grid.c2, HD), F32),
            pltpu.VMEM((all_rows, HD), F32),
            pltpu.VMEM((all_blocks, width), BF16),
            pltpu.VMEM((all_rows, width), BF16),
            pltpu.VMEM((all_rows, width), BF16),
            dma((grid.nb,)),
            dma((grid.nb,)),
            dma((grid.nu,)),
            dma((grid.nu,)),
            dma((grid.nb,)),
            dma((grid.nb,)),
        ],
        compiler_params=pltpu.CompilerParams(collective_id=0, has_side_effects=True),
    )(cache, prompt_order, response_prompt)
    out, dq, dk, dv, terms = attend(
        response_length, response_query[0], out_grad[0], response_kv[0, :, 0], response_kv[0, :, 1], rows
    )
    summed = pl.pallas_call(
        functools.partial(reduce_kernel, grid),
        out_shape=jax.ShapeDtypeStruct((grid.nt, grid.c1, width), BF16),
        in_specs=[vmem, vmem],
        out_specs=vmem,
        scratch_shapes=[
            pltpu.VMEM((all_rows, width), BF16),
            pltpu.VMEM((all_rows, width), BF16),
            pltpu.VMEM((all_blocks, width), BF16),
            pltpu.VMEM((all_blocks, width), BF16),
            dma((grid.nb,)),
            dma((grid.nb,)),
            dma((grid.nu,)),
            dma((grid.nu,)),
        ],
        compiler_params=pltpu.CompilerParams(collective_id=1, has_side_effects=True),
    )(terms, pick)
    prompt_cache_grad = summed.transpose(1, 0, 2).reshape(prompt_cache.shape)
    return (out[None], dq[None], jnp.stack([dk, dv], 1)[None], prompt_cache_grad)


def solution(mesh):
    grid = Grid(mesh.shape["seq"], mesh.shape["tp"], 16)
    return jax.shard_map(
        functools.partial(local, grid),
        mesh=mesh,
        in_specs=(
            P("seq", None, "tp"),
            P("seq", None, None, "tp"),
            P("seq", "tp", None, None),
            P(),
            P("seq"),
            P("seq"),
            P("seq", None, "tp"),
        ),
        out_specs=(
            P("seq", None, "tp"),
            P("seq", None, "tp"),
            P("seq", None, None, "tp"),
            P("seq", "tp", None, None),
        ),
        check_vma=False,
    )
```

time: 946 us -> 94.8 us (0.10)
  waiting for transfers between devices: 769 us -> 0 us
  Pallas kernels: 0 us -> 81.7 us
  matrix products: 78.7 us -> 0 us
  other arithmetic: 27.2 us -> 1.3 us
  local copies, waits for them, and re-layouts: 33.4 us -> 9.46 us
  between operations: 17.5 us -> 1.96 us
    reduce_scatter x1 -> x0, waiting for transfers between devices: 570 us -> none  [local(): summed = lax.psum_scatter(dense, 'seq', scatter_dimension=0, tiled=True)]
    all_gather x1 -> x0, waiting for transfers between devices: 198 us -> none  [local(): everything = lax.all_gather(halves, 'seq', axis=0, tiled=True)]
    pallas_call x0 -> x3, Pallas kernels: none -> 81.7 us  [the longest x1 29.1 us: attend(): pl.pallas_call(attend_kernel, out_shape=(jax.ShapeDtypeStruct(q.shape, BF...]
    dot_general x20 -> x0, matrix products: 52.9 us -> none  [the longest x4 17.4 us: head_step(): jnp.einsum('tgd,ld->gtl', grad_live, value_rows, preferred_element_type=j...]
    sub x4 -> x0, matrix products: 25.8 us -> none  [head_step(): raised = jnp.exp(scores - highest)]
    unnamed x19 -> x1, local copies, waits for them, and re-layouts: 21.7 us -> 2.05 us
    convert_element_type x9 -> x0, other arithmetic: 11 us -> none  [the longest x4 7.55 us: head_step(): dscores = (probs * (dprobs - center)).astype(jnp.bfloat16)]
  transfers between devices with their start and end apart: 3 -> 0, of which waited for: 2 -> 0; matrix products, arithmetic and copies ran while one was open for 3% -> 0% of each run, Pallas kernels for 0% -> 0%
where the time goes in v1:
time: 94.8 us; the launch traced here: 94.4 us
  Pallas kernels  81.7 us (86%)
  local copies, waits for them, and re-layouts  9.46 us (10%)
  between operations  1.96 us (2%)
  other arithmetic  1.3 us (1%)
    pallas_call x1, Pallas kernels, attend(): pl.pallas_call(attend_kernel, out_shape=(jax.ShapeDtypeStruct(q.shape, BF...  29.1 us
    pallas_call x1, Pallas kernels, local(): pl.pallas_call(functools.partial(gather_kernel, grid), out_shape=(jax.Sha...  27.7 us
    pallas_call x1, Pallas kernels, local(): pl.pallas_call(functools.partial(reduce_kernel, grid), out_shape=jax.Shap...  24.9 us
    slice x1, local copies, waits for them, and re-layouts, local(): response_kv[0, :, 1]  3.3 us
    unnamed x1, local copies, waits for them, and re-layouts  2.05 us

profile of v1, /device:TPU:1, one launch (start us, length us, event | category | flops | bytes accessed | tf_op | source)
XLA Modules:
  0.0 94.4 jit_solution(13316156557943509553)
XLA Ops:
  1.9 0.8 reshape.14
  2.7 0.6 copy.24
  3.3 27.7 %shard_map.102 = (bf16[256,512]{1,0:T(8,128)(2,1)}, bf16[256,256]{1,0:T(8,128)(2,1)}) custom-call(bf16[2,16,512]{2,1,0:T(8,128)(2,1)} %bitcast.20, s32[16]{0:T(128)} %order_ref.1, s32[1]{0:T(128)S(6)} %copy.25.owner_ref), custom_call_target="tpu_custom_call" | custom-call | tf_op jit(solution)/shard_map/pallas_call | solution.py:447
  31.0 3.3 %fusion = (bf16[1,512,1,512]{3,2,1,0:T(2,128)(2,1)S(1)}, bf16[1,512,1,512]{3,2,1,0:T(2,128)(2,1)S(1)}) fusion(bf16[1,512,2,512]{3,2,1,0:T(2,128)(2,1)} %param.8), kind=kLoop, calls=%fused_computation.4 | loop fusion | bytes 2097152 | tf_op jit(solution)/shard_map/slice | solution.py:471
  34.3 1.3 %copy_bitcast_fusion = (bf16[512,512]{1,0:T(8,128)(2,1)}, bf16[512,512]{1,0:T(8,128)(2,1)}) fusion(bf16[1,512,1,512]{3,2,1,0:T(2,128)(2,1)S(1)} %get-tuple-element.26, bf16[1,512,1,512]{3,2,1,0:T(2,128)(2,1)S(1)} %get-tuple-element.27), kind=kLoop, calls=%fused_computation.1 | loop fusion | bytes 2097152 | tf_op jit(solution)/shard_map/squeeze | solution.py:471
  35.6 29.1 %shard_map.103 = (bf16[512,2560]{1,0:T(8,128)(2,1)}, bf16[512,2560]{1,0:T(8,128)(2,1)}, bf16[512,512]{1,0:T(8,128)(2,1)}, bf16[512,512]{1,0:T(8,128)(2,1)}, bf16[256,512]{1,0:T(8,128)(2,1)}) custom-call(s32[1]{0:T(128)S(6)} %copy.26.length_ref, bf16[512,2560]{1,0:T(8,128)(2,1)} %bitcast.16, bf16[512,2560]{1,0:T(8,128)(2,1)} %bitcast.17, ...), custom_call_target="tpu_custom_call" | custom-call | tf_op jit(solution)/shard_map/pallas_call | solution.py:403
  64.7 24.9 %shard_map.104 = bf16[2,16,512]{2,1,0:T(8,128)(2,1)} custom-call(bf16[256,512]{1,0:T(8,128)(2,1)} %get-tuple-element.16.terms_ref, bf16[256,256]{1,0:T(8,128)(2,1)} %get-tuple-element.17.pick_ref), custom_call_target="tpu_custom_call" | custom-call | tf_op jit(solution)/shard_map/pallas_call | solution.py:473
  89.6 0.8 copy.17
  90.4 0.6 reshape.15
  91.0 1.3 %maximum_bitcast_fusion = bf16[1,512,2,512]{3,1,2,0:T(8,128)(2,1)S(1)} fusion(bf16[512,1,512]{2,0,1:T(8,128)(2,1)} %bitcast.19, bf16[512,1,512]{2,0,1:T(8,128)(2,1)} %bitcast.18), kind=kLoop, calls=%fused_computation | loop fusion | flops 524288 | bytes 2097152 | tf_op jit(solution)/shard_map/broadcast_in_dim | solution.py:491
  92.3 2.0 %copy.18 = bf16[1,512,2,512]{3,2,1,0:T(2,128)(2,1)} copy(bf16[1,512,2,512]{3,1,2,0:T(8,128)(2,1)S(1)} %maximum_bitcast_fusion) | data formatting | bytes 2097152

commit v2 on v1

v2 whole, which is shorter than its diff:
```python
import functools
import math

import jax
import jax.numpy as jnp
from jax import lax
from jax.experimental import pallas as pl
from jax.experimental.pallas import tpu as pltpu
from jax.sharding import PartitionSpec as P

HQ = 40
KVH = 8
HD = 128
PLEN = 128
RMAX = 512
GROUP = HQ // KVH
ROWS = 128
TILES = RMAX // ROWS
STACK = GROUP * ROWS
STARTS = (0, 128, 384, 768)
WIDE = 1280
SCALE = 1.0 / math.sqrt(HD)
LOG2 = SCALE * math.log2(math.e)
F32 = jnp.float32
BF16 = jnp.bfloat16
MESH = pl.DeviceIdType.MESH


def dot_nn(a, b):
    return lax.dot_general(a, b, (((1,), (0,)), ((), ())), preferred_element_type=F32)


def dot_nt(a, b):
    return lax.dot_general(a, b, (((1,), (1,)), ((), ())), preferred_element_type=F32)


def dot_tn(a, b):
    return lax.dot_general(a, b, (((0,), (0,)), ((), ())), preferred_element_type=F32)


class Grid:
    def __init__(self, seq, tp, blocks):
        self.nb = 16 if seq >= 128 else 4
        self.na = seq // self.nb
        self.nt = tp
        self.nu = self.na * tp
        self.bl = blocks // tp
        self.c1 = self.bl * 2
        self.c2 = self.na * 2

    def here(self):
        seq, t = lax.axis_index("seq"), lax.axis_index("tp")
        a, b = seq // self.nb, lax.rem(seq, self.nb)
        return a, b, t, a * self.nt + t

    def plane(self, u, b):
        return {"seq": (u // self.nt) * self.nb + b, "tp": lax.rem(u, self.nt)}

    def column(self, a, b, t):
        return {"seq": a * self.nb + b, "tp": t}


def greet(grid):
    a, b, t, u = grid.here()
    barrier = pltpu.get_barrier_semaphore()

    def plane(o, carry):
        peer = lax.rem(u + o, grid.nu)
        pl.semaphore_signal(barrier, inc=1, device_id=grid.plane(peer, b), device_id_type=MESH)
        return carry

    def column(o, carry):
        peer = lax.rem(b + o, grid.nb)
        pl.semaphore_signal(barrier, inc=1, device_id=grid.column(a, peer, t), device_id_type=MESH)
        return carry

    lax.fori_loop(1, grid.nu, plane, 0)
    lax.fori_loop(1, grid.nb, column, 0)
    pl.semaphore_wait(barrier, grid.nu + grid.nb - 2)


def plane_copy(grid, o, source, target, send, recv):
    a, b, t, u = grid.here()
    peer = lax.rem(u + o, grid.nu)
    return pltpu.make_async_remote_copy(
        src_ref=source(peer),
        dst_ref=target(u),
        send_sem=send.at[o],
        recv_sem=recv.at[o],
        device_id=grid.plane(peer, b),
        device_id_type=MESH,
    )


def column_copy(grid, o, source, target, send, recv):
    a, b, t, u = grid.here()
    peer = lax.rem(b + o, grid.nb)
    return pltpu.make_async_remote_copy(
        src_ref=source(peer),
        dst_ref=target(b),
        send_sem=send.at[o],
        recv_sem=recv.at[o],
        device_id=grid.column(a, peer, t),
        device_id_type=MESH,
    )


def start_all(copy, count):
    def step(o, carry):
        copy(o).start()
        return carry

    lax.fori_loop(1, count, step, 0)


def wait_recv_all(copy, count):
    def step(o, carry):
        copy(o).wait_recv()
        return carry

    lax.fori_loop(1, count, step, 0)


def wait_send_all(copy, count):
    def step(o, carry):
        copy(o).wait_send()
        return carry

    lax.fori_loop(1, count, step, 0)


def chunk(ref, size):
    return lambda i: ref.at[pl.ds(pl.multiple_of(i * size, size), size)]


def choice(grid, picks):
    rows, cols = grid.nb * grid.c2, grid.nu * grid.c1
    row = lax.broadcasted_iota(jnp.int32, (rows, cols), 0)
    col = lax.broadcasted_iota(jnp.int32, (rows, cols), 1)
    inner = row % grid.c2
    kv, a = inner // grid.na, inner % grid.na
    wanted = a * (grid.nt * grid.c1) + picks.astype(jnp.int32) * 2 + kv
    return jnp.where(col == wanted, 1.0, 0.0).astype(BF16)


def shuffle(grid):
    rows = grid.nb * grid.c2
    row = lax.broadcasted_iota(jnp.int32, (rows, rows), 0)
    col = lax.broadcasted_iota(jnp.int32, (rows, rows), 1)
    half = grid.nb * grid.na
    kv, b, a = row // half, (row % half) // grid.na, row % grid.na
    return jnp.where(col == b * grid.c2 + kv * grid.na + a, 1.0, 0.0).astype(BF16)


def pairs():
    row = lax.broadcasted_iota(jnp.int32, (2 * ROWS, 2 * ROWS), 0)
    col = lax.broadcasted_iota(jnp.int32, (2 * ROWS, 2 * ROWS), 1)
    return jnp.where(col == (row % ROWS) * 2 + row // ROWS, 1.0, 0.0).astype(BF16)


def kernel(
    grid,
    order_ref,
    owner_ref,
    length_ref,
    cache_ref,
    kv_ref,
    q_hbm,
    g_hbm,
    out_hbm,
    dq_hbm,
    dkv_ref,
    cgrad_ref,
    mark,
    marks,
    first,
    pick,
    chosen,
    second,
    rows,
    terms,
    outgoing,
    third,
    dense,
    fourth,
    q_buf,
    g_buf,
    out_buf,
    dq_buf,
    k_own,
    v_own,
    scores,
    raised,
    memo_o,
    memo_l,
    memo_m,
    front,
    sum_k,
    sum_v,
    in_sem,
    out_sem,
    send_m,
    recv_m,
    send_1,
    recv_1,
    send_2,
    recv_2,
    send_3,
    recv_3,
    send_4,
    recv_4,
):
    a, b, t, u = grid.here()
    heads = q_buf.shape[0]
    width = k_own.shape[1]
    half = width // 2
    length = length_ref[0]

    def moved(kv):
        return pl.ds(pl.multiple_of(kv * STACK, STACK), STACK)

    def load_q(kv):
        return pltpu.make_async_copy(q_hbm.at[:, moved(kv)], q_buf.at[kv], in_sem.at[0, kv])

    def load_g(kv):
        return pltpu.make_async_copy(g_hbm.at[:, moved(kv)], g_buf.at[kv], in_sem.at[1, kv])

    def save_out(kv):
        return pltpu.make_async_copy(out_buf.at[kv], out_hbm.at[:, moved(kv)], out_sem.at[0, kv])

    def save_dq(kv):
        return pltpu.make_async_copy(dq_buf.at[kv], dq_hbm.at[:, moved(kv)], out_sem.at[1, kv])

    def stacked(ref, kv, i):
        return jnp.concatenate(
            [ref[kv, i * ROWS : (i + 1) * ROWS, h * HD : (h + 1) * HD] for h in range(GROUP)], 0
        )

    def lanes(kv):
        return pl.ds(pl.multiple_of(kv * HD, HD), HD)

    tri = lax.broadcasted_iota(jnp.int32, (ROWS, ROWS), 1) <= lax.broadcasted_iota(jnp.int32, (ROWS, ROWS), 0)
    rows_at = lax.broadcasted_iota(jnp.int32, (ROWS, HD), 0)

    def own_forward(kv, carry):
        load_q(kv).wait()
        for i in range(TILES):
            seen = (i + 1) * ROWS
            base = STARTS[i]
            scores[:, base : base + seen] = dot_nt(stacked(q_buf, kv, i), k_own[:seen, lanes(kv)])
            for h in range(GROUP):
                part = slice(h * ROWS, (h + 1) * ROWS)
                own = [scores[part, base + j * ROWS : base + (j + 1) * ROWS] for j in range(i + 1)]
                own[i] = jnp.where(tri, own[i], -1e30)
                top = own[0]
                for piece in own[1:]:
                    top = jnp.maximum(top, piece)
                top = jnp.max(top, axis=-1, keepdims=True)
                memo_m[kv, i, part] = jnp.broadcast_to(top, (ROWS, HD))
                for j in range(i + 1):
                    raised[kv, part, base + j * ROWS : base + (j + 1) * ROWS] = jnp.exp2(
                        (own[j] - top) * LOG2
                    ).astype(BF16)
            both = jnp.concatenate([v_own[:seen, lanes(kv)], jnp.ones((seen, HD), BF16)], 1)
            result = dot_nn(raised[kv, :, base : base + seen], both)
            memo_o[kv, i] = result[:, :HD]
            memo_l[kv, i] = result[:, HD:]
        return carry

    def prompt_part(kv, carry):
        load_g(kv).wait()
        front_k = rows[:PLEN, lanes(kv)]
        front_v = rows[PLEN:, lanes(kv)]
        both = jnp.concatenate([front_v, jnp.ones((PLEN, HD), BF16)], 1)
        term_k = jnp.zeros((PLEN, HD), F32)
        term_v = jnp.zeros((PLEN, HD), F32)
        for i in range(TILES):
            query = stacked(q_buf, kv, i)
            grad = stacked(g_buf, kv, i)
            first_s = dot_nt(query, front_k)
            first_dp = dot_nt(grad, front_v)
            first_e, alphas = [], []
            for h in range(GROUP):
                part = slice(h * ROWS, (h + 1) * ROWS)
                own_top = memo_m[kv, i, part]
                top = jnp.maximum(jnp.max(first_s[part], axis=-1, keepdims=True), own_top)
                first_e.append(jnp.exp2((first_s[part] - top) * LOG2).astype(BF16))
                alphas.append(jnp.exp2((own_top - top) * LOG2))
            first_e = jnp.concatenate(first_e, 0)
            result = dot_nn(first_e, both)
            live = rows_at + i * ROWS < length
            first_d, new_q, new_g = [], [], []
            for h in range(GROUP):
                part = slice(h * ROWS, (h + 1) * ROWS)
                alpha = alphas[h]
                total = alpha * memo_l[kv, i, part] + result[part, HD:]
                inv = jnp.where(live, 1.0 / total, 0.0)
                value = (alpha * memo_o[kv, i, part] + result[part, :HD]) * inv
                out_buf[kv, i * ROWS : (i + 1) * ROWS, h * HD : (h + 1) * HD] = value.astype(BF16)
                gf = grad[part].astype(F32)
                mid = jnp.broadcast_to(jnp.sum(gf * value, axis=-1, keepdims=True), (ROWS, HD))
                memo_l[kv, i, part] = mid
                memo_o[kv, i, part] = inv
                memo_m[kv, i, part] = alpha * inv
                new_q.append((query[part].astype(F32) * (inv * SCALE)).astype(BF16))
                new_g.append((gf * inv).astype(BF16))
                first_d.append((first_e[part].astype(F32) * (first_dp[part] - mid)).astype(BF16))
            first_d = jnp.concatenate(first_d, 0)
            front[kv, i] = first_d
            term_k = term_k + dot_tn(first_d, jnp.concatenate(new_q, 0))
            term_v = term_v + dot_tn(first_e, jnp.concatenate(new_g, 0))
        terms[:PLEN, lanes(kv)] = term_k.astype(BF16)
        terms[PLEN:, lanes(kv)] = term_v.astype(BF16)
        save_out(kv).start()
        return carry

    def own_backward(kv, carry):
        front_k = rows[:PLEN, lanes(kv)]
        sum_k[...] = jnp.zeros_like(sum_k)
        sum_v[...] = jnp.zeros_like(sum_v)
        for i in range(TILES):
            seen = (i + 1) * ROWS
            base = STARTS[i]
            scores[:, base : base + seen] = dot_nt(stacked(g_buf, kv, i), v_own[:seen, lanes(kv)])
            own_d = jnp.concatenate(
                [
                    jnp.concatenate(
                        [
                            (
                                raised[kv, h * ROWS : (h + 1) * ROWS, base + j * ROWS : base + (j + 1) * ROWS].astype(
                                    F32
                                )
                                * (
                                    scores[h * ROWS : (h + 1) * ROWS, base + j * ROWS : base + (j + 1) * ROWS]
                                    - memo_l[kv, i, h * ROWS : (h + 1) * ROWS]
                                )
                            ).astype(BF16)
                            for h in range(GROUP)
                        ],
                        0,
                    )
                    for j in range(i + 1)
                ],
                1,
            )
            factor = memo_m[kv, i]
            new_q = (stacked(q_buf, kv, i).astype(F32) * (factor * SCALE)).astype(BF16)
            new_g = (stacked(g_buf, kv, i).astype(F32) * factor).astype(BF16)
            grad_q = dot_nn(front[kv, i], front_k) * (memo_o[kv, i] * SCALE)
            grad_q = grad_q + dot_nn(own_d, k_own[:seen, lanes(kv)]) * (factor * SCALE)
            for h in range(GROUP):
                dq_buf[kv, i * ROWS : (i + 1) * ROWS, h * HD : (h + 1) * HD] = grad_q[
                    h * ROWS : (h + 1) * ROWS
                ].astype(BF16)
            sum_k[:seen] += dot_tn(own_d, new_q)
            sum_v[:seen] += dot_tn(raised[kv, :, base : base + seen], new_g)
        order = pairs()
        for j in range(TILES):
            at = slice(j * ROWS, (j + 1) * ROWS)
            dkv_ref[2 * j * ROWS : 2 * (j + 1) * ROWS, lanes(kv)] = dot_tn(
                order, jnp.concatenate([sum_k[at].astype(BF16), sum_v[at].astype(BF16)], 0)
            ).astype(BF16)
        save_dq(kv).start()
        return carry

    def run(step, low, high):
        lax.fori_loop(low, high, step, 0)

    def first_copy(o):
        return plane_copy(
            grid,
            o,
            lambda peer: cache_ref.at[
                :, pl.ds(pl.multiple_of(lax.rem(peer, grid.nt) * width, width), width)
            ],
            chunk(first, grid.c1),
            send_1,
            recv_1,
        )

    def mark_copy(o):
        return column_copy(grid, o, lambda peer: mark, chunk(marks, grid.c2), send_m, recv_m)

    def second_copy(o):
        return column_copy(grid, o, chunk(chosen, grid.c2), chunk(second, grid.c2), send_2, recv_2)

    def third_copy(part):
        return lambda o: column_copy(
            grid,
            o,
            chunk(outgoing.at[part], grid.c2),
            chunk(third.at[part], grid.c2),
            send_3.at[part],
            recv_3.at[part],
        )

    def fourth_copy(part):
        return lambda o: plane_copy(
            grid,
            o,
            chunk(dense.at[part], grid.c1),
            chunk(fourth.at[part], grid.c1),
            send_4.at[part],
            recv_4.at[part],
        )

    in_plane = pl.ds(pl.multiple_of(u * grid.c1, grid.c1), grid.c1)
    in_column = pl.ds(pl.multiple_of(b * grid.c2, grid.c2), grid.c2)

    def send_terms(part):
        outgoing[part] = dot_tn(shuffle(grid), terms[:, part * half : (part + 1) * half]).astype(BF16)
        start_all(third_copy(part), grid.nb)
        third[part, in_column] = outgoing[part, in_column]

    def send_sums(part):
        wait_recv_all(third_copy(part), grid.nb)
        dense[part] = dot_tn(pick[...], third[part]).astype(BF16)
        start_all(fourth_copy(part), grid.nu)
        fourth[part, in_plane] = dense[part, in_plane]

    def finish(part):
        wait_recv_all(fourth_copy(part), grid.nu)
        for at_t in range(grid.nt):
            total = jnp.zeros((grid.c1, half), F32)
            for at in range(at_t, grid.nu, grid.nt):
                total = total + fourth[part, at * grid.c1 : (at + 1) * grid.c1].astype(F32)
            cgrad_ref[:, at_t * width + part * half : at_t * width + (part + 1) * half] = total.astype(BF16)

    def load_all(kv, carry):
        load_q(kv).start()
        load_g(kv).start()
        return carry

    run(load_all, 0, heads)
    block = jnp.int32(0)
    for i in range(order_ref.shape[0]):
        block = block + jnp.where(order_ref[i] == owner_ref[0], i, 0)
    mark[...] = jnp.full(mark.shape, block.astype(F32), F32)
    greet(grid)
    start_all(first_copy, grid.nu)
    start_all(mark_copy, grid.nb)
    first[in_plane] = cache_ref[:, pl.ds(pl.multiple_of(t * width, width), width)]
    marks[in_column] = mark[...]
    order = pairs()
    for j in range(TILES):
        split = dot_nn(order, kv_ref[2 * j * ROWS : 2 * (j + 1) * ROWS]).astype(BF16)
        k_own[j * ROWS : (j + 1) * ROWS] = split[:ROWS]
        v_own[j * ROWS : (j + 1) * ROWS] = split[ROWS:]
    run(own_forward, 0, 2)
    wait_recv_all(mark_copy, grid.nb)
    many = grid.nu * grid.c1 // marks.shape[1]
    pick[...] = choice(
        grid, jnp.concatenate([marks[...]] * many, 1) if many > 1 else marks[:, : grid.nu * grid.c1]
    )
    wait_recv_all(first_copy, grid.nu)
    chosen[...] = dot_nn(pick[...], first[...]).astype(BF16)
    start_all(second_copy, grid.nb)
    second[in_column] = chosen[in_column]
    run(own_forward, 2, heads)
    wait_recv_all(second_copy, grid.nb)
    rows[...] = dot_nn(shuffle(grid), second[...]).astype(BF16)
    run(prompt_part, 0, heads // 2)
    send_terms(0)
    run(prompt_part, heads // 2, heads)
    send_terms(1)
    run(own_backward, 0, 1)
    send_sums(0)
    run(own_backward, 1, 2)
    send_sums(1)
    run(own_backward, 2, heads)
    finish(0)
    finish(1)

    wait_send_all(first_copy, grid.nu)
    wait_send_all(mark_copy, grid.nb)
    wait_send_all(second_copy, grid.nb)
    for part in range(2):
        wait_send_all(third_copy(part), grid.nb)
        wait_send_all(fourth_copy(part), grid.nu)

    def saved(kv, carry):
        save_out(kv).wait()
        save_dq(kv).wait()
        return carry

    run(saved, 0, heads)


def local(
    grid,
    response_query,
    response_kv,
    prompt_cache,
    prompt_order,
    response_prompt,
    response_length,
    out_grad,
):
    width = response_kv.shape[3]
    heads = width // HD
    half = width // 2
    vmem = pl.BlockSpec(memory_space=pltpu.VMEM)
    smem = pl.BlockSpec(memory_space=pltpu.SMEM)
    hbm = pl.BlockSpec(memory_space=pl.ANY)
    dma = pltpu.SemaphoreType.DMA
    all_rows = grid.nb * grid.c2
    all_blocks = grid.nu * grid.c1
    stack = (heads, TILES, STACK, HD)
    full = (heads, RMAX, STACK)
    flat = response_query.shape[1:]
    out, dq, dkv, summed = pl.pallas_call(
        functools.partial(kernel, grid),
        out_shape=(
            jax.ShapeDtypeStruct(flat, BF16),
            jax.ShapeDtypeStruct(flat, BF16),
            jax.ShapeDtypeStruct((2 * RMAX, width), BF16),
            jax.ShapeDtypeStruct((grid.c1, grid.nt * width), BF16),
        ),
        in_specs=[smem] * 3 + [vmem] * 2 + [hbm] * 2,
        out_specs=(hbm, hbm, vmem, vmem),
        scratch_shapes=[
            pltpu.VMEM((grid.c2, HD), F32),
            pltpu.VMEM((all_rows, HD), F32),
            pltpu.VMEM((all_blocks, width), BF16),
            pltpu.VMEM((all_rows, all_blocks), BF16),
            pltpu.VMEM((all_rows, width), BF16),
            pltpu.VMEM((all_rows, width), BF16),
            pltpu.VMEM((all_rows, width), BF16),
            pltpu.VMEM((all_rows, width), BF16),
            pltpu.VMEM((2, all_rows, half), BF16),
            pltpu.VMEM((2, all_rows, half), BF16),
            pltpu.VMEM((2, all_blocks, half), BF16),
            pltpu.VMEM((2, all_blocks, half), BF16),
            pltpu.VMEM(full, BF16),
            pltpu.VMEM(full, BF16),
            pltpu.VMEM(full, BF16),
            pltpu.VMEM(full, BF16),
            pltpu.VMEM((RMAX, width), BF16),
            pltpu.VMEM((RMAX, width), BF16),
            pltpu.VMEM((STACK, WIDE), F32),
            pltpu.VMEM((heads, STACK, WIDE), BF16),
            pltpu.VMEM(stack, F32),
            pltpu.VMEM(stack, F32),
            pltpu.VMEM(stack, F32),
            pltpu.VMEM(stack, BF16),
            pltpu.VMEM((RMAX, HD), F32),
            pltpu.VMEM((RMAX, HD), F32),
            dma((2, heads)),
            dma((2, heads)),
            dma((grid.nb,)),
            dma((grid.nb,)),
            dma((grid.nu,)),
            dma((grid.nu,)),
            dma((grid.nb,)),
            dma((grid.nb,)),
            dma((2, grid.nb)),
            dma((2, grid.nb)),
            dma((2, grid.nu)),
            dma((2, grid.nu)),
        ],
        compiler_params=pltpu.CompilerParams(
            collective_id=0, has_side_effects=True, vmem_limit_bytes=62 * 1024 * 1024
        ),
    )(
        prompt_order,
        response_prompt,
        response_length,
        prompt_cache.reshape(grid.c1, grid.nt * width),
        response_kv.reshape(2 * RMAX, width),
        response_query[0],
        out_grad[0],
    )
    return (out[None], dq[None], dkv.reshape(response_kv.shape), summed.reshape(prompt_cache.shape))


def solution(mesh):
    grid = Grid(mesh.shape["seq"], mesh.shape["tp"], 16)
    return jax.shard_map(
        functools.partial(local, grid),
        mesh=mesh,
        in_specs=(
            P("seq", None, "tp"),
            P("seq", None, None, "tp"),
            P("seq", "tp", None, None),
            P(),
            P("seq"),
            P("seq"),
            P("seq", None, "tp"),
        ),
        out_specs=(
            P("seq", None, "tp"),
            P("seq", None, "tp"),
            P("seq", None, None, "tp"),
            P("seq", "tp", None, None),
        ),
        check_vma=False,
    )
```

time: 94.8 us -> 70.6 us (0.74)
  Pallas kernels: 81.7 us -> 56.1 us
  local copies, waits for them, and re-layouts: 9.46 us -> 12.3 us
  other arithmetic: 1.3 us -> 0 us
    pallas_call x3 -> x1, Pallas kernels: 81.7 us -> 56.1 us  [local(): pl.pallas_call(functools.partial(kernel, grid), out_shape=(jax.ShapeDtype...]
    reshape x3 -> x4, local copies, waits for them, and re-layouts: 2.05 us -> 7.27 us  [the longest x1 2.24 us: local(): response_kv.reshape(2 * RMAX, width)]
    slice x1 -> x0, local copies, waits for them, and re-layouts: 3.3 us -> none  [local(): response_kv[0, :, 1]]
    unnamed x1 -> x4, local copies, waits for them, and re-layouts: 2.05 us -> 5.05 us
    broadcast_in_dim x1 -> x0, other arithmetic: 1.3 us -> none  [local(): jnp.stack([dk, dv], 1)[None]]
    squeeze x1 -> x0, local copies, waits for them, and re-layouts: 1.26 us -> none  [local(): response_kv[0, :, 1]]
where the time goes in v2:
time: 70.6 us; the launch traced here: 70.3 us
  Pallas kernels  56.1 us (79%)
  local copies, waits for them, and re-layouts  12.3 us (17%)
  between operations  1.94 us (3%)
    pallas_call x1, Pallas kernels, local(): pl.pallas_call(functools.partial(kernel, grid), out_shape=(jax.ShapeDtype...  56.1 us
    unnamed x4, local copies, waits for them, and re-layouts  5.05 us
    reshape x1, local copies, waits for them, and re-layouts, local(): response_kv.reshape(2 * RMAX, width)  2.24 us
    reshape x1, local copies, waits for them, and re-layouts, local(): dkv.reshape(response_kv.shape)  2.24 us

profile of v2, /device:TPU:1, one launch (start us, length us, event | category | flops | bytes accessed | tf_op | source)
XLA Modules:
  0.0 70.3 jit_solution(4592664042019440942)
XLA Ops:
  1.9 1.4 %reshape.20.cache_ref = bf16[16,1024]{1,0:T(8,128)(2,1)} reshape(bf16[1,8,2,1024]{3,2,1,0:T(2,128)(2,1)} %param.9) | data formatting | bytes 65536 | tf_op jit(solution)/shard_map/reshape | solution.py:568
  3.3 2.2 %reshape.21.kv_ref = bf16[1024,512]{1,0:T(8,128)(2,1)} reshape(bf16[1,512,2,512]{3,2,1,0:T(2,128)(2,1)} %param.8) | data formatting | bytes 2097152 | tf_op jit(solution)/shard_map/reshape | solution.py:569
  5.6 56.1 %shard_map.102 = (bf16[512,2560]{1,0:T(8,128)(2,1)}, bf16[512,2560]{1,0:T(8,128)(2,1)}, bf16[1024,512]{1,0:T(8,128)(2,1)}, bf16[16,1024]{1,0:T(8,128)(2,1)}) custom-call(s32[16]{0:T(128)} %order_ref.1, s32[1]{0:T(128)S(6)} %copy.13.owner_ref, s32[1]{0:T(128)S(6)} %copy.14.length_ref, bf16[16,1024]{1,0:T(8,128)(2,1)} %reshape.20.cache_ref, ...), custom_call_target="tpu_custom_call" | custom-call | tf_op jit(solution)/shard_map/pallas_call | solution.py:511
  61.6 1.4 %reshape.23 = bf16[1,8,2,1024]{3,2,1,0:T(2,128)(2,1)} reshape(bf16[16,1024]{1,0:T(8,128)(2,1)} %get-tuple-element.11) | data formatting | bytes 65536 | tf_op jit(solution)/shard_map/reshape | solution.py:573
  63.0 2.2 %reshape.22 = bf16[1,512,2,512]{3,2,1,0:T(2,128)(2,1)} reshape(bf16[1024,512]{1,0:T(8,128)(2,1)} %get-tuple-element.10) | data formatting | bytes 2097152 | tf_op jit(solution)/shard_map/reshape | solution.py:573
  65.3 0.0 copy-start
  65.3 3.6 %copy.15 = bf16[1,512,2560]{2,1,0:T(8,128)(2,1)} copy(bf16[1,512,2560]{2,1,0:T(8,128)(2,1)} %bitcast.7) | data formatting | bytes 5242880
  68.8 0.0 copy-done
  68.8 1.5 %copy.16 = bf16[1,512,2560]{2,1,0:T(8,128)(2,1)} copy(bf16[1,512,2560]{2,1,0:T(8,128)(2,1)S(1)} %bitcast.6) | data formatting | bytes 5242880
Async XLA Ops:
  65.3 3.6 %copy-start = (bf16[512,2560]{1,0:T(8,128)(2,1)S(1)}, bf16[512,2560]{1,0:T(8,128)(2,1)}, u32[]{:S(2)}) copy-start(bf16[512,2560]{1,0:T(8,128)(2,1)} %get-tuple-element.9) | copy-start | bytes 7864324

commit v3 on v2

--- a/solution.py
+++ b/solution.py
@@ -167,10 +167,11 @@
     kv_ref,
     q_hbm,
     g_hbm,
-    out_hbm,
-    dq_hbm,
+    out_ref,
+    dq_ref,
     dkv_ref,
     cgrad_ref,
+    cache,
     mark,
     marks,
     first,
@@ -185,20 +186,18 @@
     fourth,
     q_buf,
     g_buf,
-    out_buf,
-    dq_buf,
     k_own,
     v_own,
-    scores,
     raised,
-    memo_o,
-    memo_l,
-    memo_m,
-    front,
+    dprobs,
+    stats,
+    front_p,
+    front_d,
+    low_p,
+    low_d,
     sum_k,
     sum_v,
     in_sem,
-    out_sem,
     send_m,
     recv_m,
     send_1,
@@ -225,12 +224,6 @@
     def load_g(kv):
         return pltpu.make_async_copy(g_hbm.at[:, moved(kv)], g_buf.at[kv], in_sem.at[1, kv])
 
-    def save_out(kv):
-        return pltpu.make_async_copy(out_buf.at[kv], out_hbm.at[:, moved(kv)], out_sem.at[0, kv])
-
-    def save_dq(kv):
-        return pltpu.make_async_copy(dq_buf.at[kv], dq_hbm.at[:, moved(kv)], out_sem.at[1, kv])
-
     def stacked(ref, kv, i):
         return jnp.concatenate(
             [ref[kv, i * ROWS : (i + 1) * ROWS, h * HD : (h + 1) * HD] for h in range(GROUP)], 0
@@ -239,138 +232,125 @@
     def lanes(kv):
         return pl.ds(pl.multiple_of(kv * HD, HD), HD)
 
-    tri = lax.broadcasted_iota(jnp.int32, (ROWS, ROWS), 1) <= lax.broadcasted_iota(jnp.int32, (ROWS, ROWS), 0)
-    rows_at = lax.broadcasted_iota(jnp.int32, (ROWS, HD), 0)
+    def head_lanes(kv, h):
+        return pl.ds(pl.multiple_of(kv * STACK + h * HD, HD), HD)
+
+    tri = lax.broadcasted_iota(jnp.int32, (ROWS, ROWS), 0) <= lax.broadcasted_iota(jnp.int32, (ROWS, ROWS), 1)
+    row_at = lax.broadcasted_iota(jnp.int32, (1, ROWS), 1)
 
     def own_forward(kv, carry):
         load_q(kv).wait()
+        load_g(kv).wait()
         for i in range(TILES):
             seen = (i + 1) * ROWS
             base = STARTS[i]
-            scores[:, base : base + seen] = dot_nt(stacked(q_buf, kv, i), k_own[:seen, lanes(kv)])
+            raised[kv, base : base + seen] = dot_nt(k_own[:seen, lanes(kv)], stacked(q_buf, kv, i))
+            dprobs[kv, base : base + seen] = dot_nt(v_own[:seen, lanes(kv)], stacked(g_buf, kv, i))
             for h in range(GROUP):
                 part = slice(h * ROWS, (h + 1) * ROWS)
-                own = [scores[part, base + j * ROWS : base + (j + 1) * ROWS] for j in range(i + 1)]
-                own[i] = jnp.where(tri, own[i], -1e30)
-                top = own[0]
-                for piece in own[1:]:
-                    top = jnp.maximum(top, piece)
-                top = jnp.max(top, axis=-1, keepdims=True)
-                memo_m[kv, i, part] = jnp.broadcast_to(top, (ROWS, HD))
-                for j in range(i + 1):
-                    raised[kv, part, base + j * ROWS : base + (j + 1) * ROWS] = jnp.exp2(
-                        (own[j] - top) * LOG2
-                    ).astype(BF16)
-            both = jnp.concatenate([v_own[:seen, lanes(kv)], jnp.ones((seen, HD), BF16)], 1)
-            result = dot_nn(raised[kv, :, base : base + seen], both)
-            memo_o[kv, i] = result[:, :HD]
-            memo_l[kv, i] = result[:, HD:]
+                blocks = [slice(base + c * ROWS, base + (c + 1) * ROWS) for c in range(i + 1)]
+                diagonal = jnp.where(tri, raised[kv, blocks[i], part], -1e30)
+                top = diagonal
+                for c in range(i):
+                    top = jnp.maximum(top, raised[kv, blocks[c], part])
+                top = jnp.max(top, axis=0, keepdims=True)
+                total = jnp.zeros((ROWS, ROWS), F32)
+                center = jnp.zeros((ROWS, ROWS), F32)
+                for c in range(i + 1):
+                    piece = diagonal if c == i else raised[kv, blocks[c], part]
+                    piece = jnp.exp2((piece - top) * LOG2)
+                    raised[kv, blocks[c], part] = piece
+                    total = total + piece
+                    center = center + piece * dprobs[kv, blocks[c], part]
+                stats[kv, i, 0:1, part] = top
+                stats[kv, i, 1:2, part] = jnp.sum(total, axis=0, keepdims=True)
+                stats[kv, i, 2:3, part] = jnp.sum(center, axis=0, keepdims=True)
         return carry
 
     def prompt_part(kv, carry):
-        load_g(kv).wait()
         front_k = rows[:PLEN, lanes(kv)]
         front_v = rows[PLEN:, lanes(kv)]
-        both = jnp.concatenate([front_v, jnp.ones((PLEN, HD), BF16)], 1)
         term_k = jnp.zeros((PLEN, HD), F32)
         term_v = jnp.zeros((PLEN, HD), F32)
         for i in range(TILES):
             query = stacked(q_buf, kv, i)
             grad = stacked(g_buf, kv, i)
-            first_s = dot_nt(query, front_k)
-            first_dp = dot_nt(grad, front_v)
-            first_e, alphas = [], []
+            scores = dot_nt(front_k, query)
+            first_dp = dot_nt(front_v, grad)
+            live = row_at + i * ROWS < length
             for h in range(GROUP):
                 part = slice(h * ROWS, (h + 1) * ROWS)
-                own_top = memo_m[kv, i, part]
-                top = jnp.maximum(jnp.max(first_s[part], axis=-1, keepdims=True), own_top)
-                first_e.append(jnp.exp2((first_s[part] - top) * LOG2).astype(BF16))
-                alphas.append(jnp.exp2((own_top - top) * LOG2))
-            first_e = jnp.concatenate(first_e, 0)
-            result = dot_nn(first_e, both)
-            live = rows_at + i * ROWS < length
-            first_d, new_q, new_g = [], [], []
-            for h in range(GROUP):
-                part = slice(h * ROWS, (h + 1) * ROWS)
-                alpha = alphas[h]
-                total = alpha * memo_l[kv, i, part] + result[part, HD:]
-                inv = jnp.where(live, 1.0 / total, 0.0)
-                value = (alpha * memo_o[kv, i, part] + result[part, :HD]) * inv
-                out_buf[kv, i * ROWS : (i + 1) * ROWS, h * HD : (h + 1) * HD] = value.astype(BF16)
-                gf = grad[part].astype(F32)
-                mid = jnp.broadcast_to(jnp.sum(gf * value, axis=-1, keepdims=True), (ROWS, HD))
-                memo_l[kv, i, part] = mid
-                memo_o[kv, i, part] = inv
-                memo_m[kv, i, part] = alpha * inv
-                new_q.append((query[part].astype(F32) * (inv * SCALE)).astype(BF16))
-                new_g.append((gf * inv).astype(BF16))
-                first_d.append((first_e[part].astype(F32) * (first_dp[part] - mid)).astype(BF16))
-            first_d = jnp.concatenate(first_d, 0)
-            front[kv, i] = first_d
-            term_k = term_k + dot_tn(first_d, jnp.concatenate(new_q, 0))
-            term_v = term_v + dot_tn(first_e, jnp.concatenate(new_g, 0))
+                own_top = stats[kv, i, 0:1, part]
+                top = jnp.maximum(jnp.max(scores[:, part], axis=0, keepdims=True), own_top)
+                alpha = jnp.exp2((own_top - top) * LOG2)
+                first_e = jnp.exp2((scores[:, part] - top) * LOG2)
+                dp = first_dp[:, part]
+                total = alpha * stats[kv, i, 1:2, part] + jnp.sum(first_e, axis=0, keepdims=True)
+                center = alpha * stats[kv, i, 2:3, part] + jnp.sum(first_e * dp, axis=0, keepdims=True)
+                inv = 1.0 / total
+                center = center * inv
+                inv = jnp.where(live, inv, 0.0)
+                stats[kv, i, 3:4, part] = alpha * inv
+                stats[kv, i, 4:5, part] = center
+                probs = first_e * inv
+                front_p[kv, i, :, part] = probs.astype(BF16)
+                front_d[kv, i, :, part] = (probs * ((dp - center) * SCALE)).astype(BF16)
+            term_k = term_k + dot_nn(front_d[kv, i], query)
+            term_v = term_v + dot_nn(front_p[kv, i], grad)
         terms[:PLEN, lanes(kv)] = term_k.astype(BF16)
         terms[PLEN:, lanes(kv)] = term_v.astype(BF16)
-        save_out(kv).start()
         return carry
 
     def own_backward(kv, carry):
         front_k = rows[:PLEN, lanes(kv)]
+        front_v = rows[PLEN:, lanes(kv)]
         sum_k[...] = jnp.zeros_like(sum_k)
         sum_v[...] = jnp.zeros_like(sum_v)
         for i in range(TILES):
             seen = (i + 1) * ROWS
             base = STARTS[i]
-            scores[:, base : base + seen] = dot_nt(stacked(g_buf, kv, i), v_own[:seen, lanes(kv)])
-            own_d = jnp.concatenate(
-                [
-                    jnp.concatenate(
-                        [
-                            (
-                                raised[kv, h * ROWS : (h + 1) * ROWS, base + j * ROWS : base + (j + 1) * ROWS].astype(
-                                    F32
-                                )
-                                * (
-                                    scores[h * ROWS : (h + 1) * ROWS, base + j * ROWS : base + (j + 1) * ROWS]
-                                    - memo_l[kv, i, h * ROWS : (h + 1) * ROWS]
-                                )
-                            ).astype(BF16)
-                            for h in range(GROUP)
-                        ],
-                        0,
-                    )
-                    for j in range(i + 1)
-                ],
-                1,
+            query = stacked(q_buf, kv, i)
+            grad = stacked(g_buf, kv, i)
+            for h in range(GROUP):
+                part = slice(h * ROWS, (h + 1) * ROWS)
+                factor = stats[kv, i, 3:4, part]
+                center = stats[kv, i, 4:5, part]
+                for c in range(i + 1):
+                    at = slice(base + c * ROWS, base + (c + 1) * ROWS)
+                    probs = raised[kv, at, part] * factor
+                    low_p[at, part] = probs.astype(BF16)
+                    low_d[at, part] = (probs * ((dprobs[kv, at, part] - center) * SCALE)).astype(BF16)
+            own_p = low_p[base : base + seen]
+            own_d = low_d[base : base + seen]
+            sum_k[:seen] += dot_nn(own_d, query)
+            sum_v[:seen] += dot_nn(own_p, grad)
+            result = dot_tn(
+                jnp.concatenate([front_p[kv, i], own_p], 0), jnp.concatenate([front_v, v_own[:seen, lanes(kv)]], 0)
             )
-            factor = memo_m[kv, i]
-            new_q = (stacked(q_buf, kv, i).astype(F32) * (factor * SCALE)).astype(BF16)
-            new_g = (stacked(g_buf, kv, i).astype(F32) * factor).astype(BF16)
-            grad_q = dot_nn(front[kv, i], front_k) * (memo_o[kv, i] * SCALE)
-            grad_q = grad_q + dot_nn(own_d, k_own[:seen, lanes(kv)]) * (factor * SCALE)
+            grad_q = dot_tn(
+                jnp.concatenate([front_d[kv, i], own_d], 0), jnp.concatenate([front_k, k_own[:seen, lanes(kv)]], 0)
+            )
             for h in range(GROUP):
-                dq_buf[kv, i * ROWS : (i + 1) * ROWS, h * HD : (h + 1) * HD] = grad_q[
-                    h * ROWS : (h + 1) * ROWS
-                ].astype(BF16)
-            sum_k[:seen] += dot_tn(own_d, new_q)
-            sum_v[:seen] += dot_tn(raised[kv, :, base : base + seen], new_g)
+                part = slice(h * ROWS, (h + 1) * ROWS)
+                out_ref[i * ROWS : (i + 1) * ROWS, head_lanes(kv, h)] = result[part].astype(BF16)
+                dq_ref[i * ROWS : (i + 1) * ROWS, head_lanes(kv, h)] = grad_q[part].astype(BF16)
         order = pairs()
-        for j in range(TILES):
-            at = slice(j * ROWS, (j + 1) * ROWS)
-            dkv_ref[2 * j * ROWS : 2 * (j + 1) * ROWS, lanes(kv)] = dot_tn(
-                order, jnp.concatenate([sum_k[at].astype(BF16), sum_v[at].astype(BF16)], 0)
-            ).astype(BF16)
-        save_dq(kv).start()
+        for c in range(TILES):
+            at = slice(c * ROWS, (c + 1) * ROWS)
+            mixed = dot_tn(order, jnp.concatenate([sum_k[at].astype(BF16), sum_v[at].astype(BF16)], 0))
+            dkv_ref[at, :, lanes(kv)] = mixed.astype(BF16).reshape(ROWS, 2, HD)
         return carry
 
     def run(step, low, high):
         lax.fori_loop(low, high, step, 0)
+
+    cache[...] = cache_ref[...].reshape(cache.shape)
 
     def first_copy(o):
         return plane_copy(
             grid,
             o,
-            lambda peer: cache_ref.at[
+            lambda peer: cache.at[
                 :, pl.ds(pl.multiple_of(lax.rem(peer, grid.nt) * width, width), width)
             ],
             chunk(first, grid.c1),
@@ -424,7 +404,9 @@
             total = jnp.zeros((grid.c1, half), F32)
             for at in range(at_t, grid.nu, grid.nt):
                 total = total + fourth[part, at * grid.c1 : (at + 1) * grid.c1].astype(F32)
-            cgrad_ref[:, at_t * width + part * half : at_t * width + (part + 1) * half] = total.astype(BF16)
+            cgrad_ref[:, :, at_t * width + part * half : at_t * width + (part + 1) * half] = total.astype(
+                BF16
+            ).reshape(grid.bl, 2, half)
 
     def load_all(kv, carry):
         load_q(kv).start()
@@ -439,11 +421,11 @@
     greet(grid)
     start_all(first_copy, grid.nu)
     start_all(mark_copy, grid.nb)
-    first[in_plane] = cache_ref[:, pl.ds(pl.multiple_of(t * width, width), width)]
+    first[in_plane] = cache[:, pl.ds(pl.multiple_of(t * width, width), width)]
     marks[in_column] = mark[...]
     order = pairs()
     for j in range(TILES):
-        split = dot_nn(order, kv_ref[2 * j * ROWS : 2 * (j + 1) * ROWS]).astype(BF16)
+        split = dot_nn(order, kv_ref[j * ROWS : (j + 1) * ROWS].reshape(2 * ROWS, width)).astype(BF16)
         k_own[j * ROWS : (j + 1) * ROWS] = split[:ROWS]
         v_own[j * ROWS : (j + 1) * ROWS] = split[ROWS:]
     run(own_forward, 0, 2)
@@ -478,12 +460,13 @@
         wait_send_all(third_copy(part), grid.nb)
         wait_send_all(fourth_copy(part), grid.nu)
 
-    def saved(kv, carry):
-        save_out(kv).wait()
-        save_dq(kv).wait()
-        return carry
-
-    run(saved, 0, heads)
+
+def hand_on(*refs):
+    copies = [pltpu.make_async_copy(refs[i], refs[4 + i], refs[8].at[i]) for i in range(4)]
+    for copy in copies:
+        copy.start()
+    for copy in copies:
+        copy.wait()
 
 
 def local(
@@ -505,7 +488,6 @@
     dma = pltpu.SemaphoreType.DMA
     all_rows = grid.nb * grid.c2
     all_blocks = grid.nu * grid.c1
-    stack = (heads, TILES, STACK, HD)
     full = (heads, RMAX, STACK)
     flat = response_query.shape[1:]
     out, dq, dkv, summed = pl.pallas_call(
@@ -513,12 +495,13 @@
         out_shape=(
             jax.ShapeDtypeStruct(flat, BF16),
             jax.ShapeDtypeStruct(flat, BF16),
-            jax.ShapeDtypeStruct((2 * RMAX, width), BF16),
-            jax.ShapeDtypeStruct((grid.c1, grid.nt * width), BF16),
+            jax.ShapeDtypeStruct((RMAX, 2, width), BF16),
+            jax.ShapeDtypeStruct((grid.bl, 2, grid.nt * width), BF16),
         ),
         in_specs=[smem] * 3 + [vmem] * 2 + [hbm] * 2,
-        out_specs=(hbm, hbm, vmem, vmem),
+        out_specs=(vmem,) * 4,
         scratch_shapes=[
+            pltpu.VMEM((grid.c1, grid.nt * width), BF16),
             pltpu.VMEM((grid.c2, HD), F32),
             pltpu.VMEM((all_rows, HD), F32),
             pltpu.VMEM((all_blocks, width), BF16),
@@ -533,19 +516,17 @@
             pltpu.VMEM((2, all_blocks, half), BF16),
             pltpu.VMEM(full, BF16),
             pltpu.VMEM(full, BF16),
-            pltpu.VMEM(full, BF16),
-            pltpu.VMEM(full, BF16),
             pltpu.VMEM((RMAX, width), BF16),
             pltpu.VMEM((RMAX, width), BF16),
-            pltpu.VMEM((STACK, WIDE), F32),
-            pltpu.VMEM((heads, STACK, WIDE), BF16),
-            pltpu.VMEM(stack, F32),
-            pltpu.VMEM(stack, F32),
-            pltpu.VMEM(stack, F32),
-            pltpu.VMEM(stack, BF16),
+            pltpu.VMEM((heads, WIDE, STACK), F32),
+            pltpu.VMEM((heads, WIDE, STACK), F32),
+            pltpu.VMEM((heads, TILES, 8, STACK), F32),
+            pltpu.VMEM((heads, TILES, PLEN, STACK), BF16),
+            pltpu.VMEM((heads, TILES, PLEN, STACK), BF16),
+            pltpu.VMEM((WIDE, STACK), BF16),
+            pltpu.VMEM((WIDE, STACK), BF16),
             pltpu.VMEM((RMAX, HD), F32),
             pltpu.VMEM((RMAX, HD), F32),
-            dma((2, heads)),
             dma((2, heads)),
             dma((grid.nb,)),
             dma((grid.nb,)),
@@ -559,18 +540,26 @@
             dma((2, grid.nu)),
         ],
         compiler_params=pltpu.CompilerParams(
-            collective_id=0, has_side_effects=True, vmem_limit_bytes=62 * 1024 * 1024
+            collective_id=0, has_side_effects=True, vmem_limit_bytes=46 * 1024 * 1024
         ),
     )(
         prompt_order,
         response_prompt,
         response_length,
-        prompt_cache.reshape(grid.c1, grid.nt * width),
-        response_kv.reshape(2 * RMAX, width),
+        prompt_cache[0],
+        response_kv[0],
         response_query[0],
         out_grad[0],
     )
-    return (out[None], dq[None], dkv.reshape(response_kv.shape), summed.reshape(prompt_cache.shape))
+    out, dq, dkv, summed = pl.pallas_call(
+        hand_on,
+        out_shape=tuple(jax.ShapeDtypeStruct(x.shape, x.dtype) for x in (out, dq, dkv, summed)),
+        in_specs=[hbm] * 4,
+        out_specs=(hbm,) * 4,
+        scratch_shapes=[dma((4,))],
+        compiler_params=pltpu.CompilerParams(vmem_limit_bytes=1024 * 1024),
+    )(out, dq, dkv, summed)
+    return (out[None], dq[None], dkv[None], summed[None])
 
 
 def solution(mesh):

time: 70.6 us -> 57.7 us (0.82)
  local copies, waits for them, and re-layouts: 12.3 us -> 2.63 us
  Pallas kernels: 56.1 us -> 52.7 us
    reshape x4 -> x0, local copies, waits for them, and re-layouts: 7.27 us -> none  [the longest x1 2.24 us: local(): response_kv.reshape(2 * RMAX, width)]
    pallas_call x1, Pallas kernels: 56.1 us -> 50 us  [local(): pl.pallas_call(functools.partial(kernel, grid), out_shape=(jax.ShapeDtype...]
    pallas_call x0 -> x1, Pallas kernels: none -> 2.73 us  [local(): pl.pallas_call(hand_on, out_shape=tuple((jax.ShapeDtypeStruct(x.shape, x....]
    unnamed x4 -> x6, local copies, waits for them, and re-layouts: 5.05 us -> 2.63 us
where the time goes in v3:
time: 57.7 us; the launch traced here: 57.5 us
  Pallas kernels  52.7 us (91%)
  local copies, waits for them, and re-layouts  2.63 us (5%)
  between operations  2.1 us (4%)
    pallas_call x1, Pallas kernels, local(): pl.pallas_call(functools.partial(kernel, grid), out_shape=(jax.ShapeDtype...  50 us
    pallas_call x1, Pallas kernels, local(): pl.pallas_call(hand_on, out_shape=tuple((jax.ShapeDtypeStruct(x.shape, x....  2.73 us
    unnamed x6, local copies, waits for them, and re-layouts  2.63 us

profile of v3, /device:TPU:1, one launch (start us, length us, event | category | flops | bytes accessed | tf_op | source)
XLA Modules:
  0.0 57.5 jit_solution(3405064110791929614)
XLA Ops:
  1.9 0.0 copy-start
  1.9 1.2 %copy-done = bf16[1,512,2,512]{3,2,1,0:T(2,128)(2,1)S(1)} copy-done((bf16[1,512,2,512]{3,2,1,0:T(2,128)(2,1)S(1)}, bf16[1,512,2,512]{3,2,1,0:T(2,128)(2,1)}, u32[]{:S(2)}) %copy-start) | copy-done | bytes 1048600
  3.1 0.0 copy-start.1
  3.2 0.8 %copy-done.1 = bf16[1,8,2,1024]{3,2,1,0:T(2,128)(2,1)S(1)} copy-done((bf16[1,8,2,1024]{3,2,1,0:T(2,128)(2,1)S(1)}, bf16[1,8,2,1024]{3,2,1,0:T(2,128)(2,1)}, u32[]{:S(2)}) %copy-start.1) | copy-done | bytes 32792
  3.9 0.0 copy-start.2
  3.9 0.7 %copy-done.2 = s32[16]{0:T(128)S(1)} copy-done((s32[16]{0:T(128)S(1)}, s32[16]{0:T(128)}, u32[]{:S(2)}) %copy-start.2) | copy-done | bytes 88
  4.6 50.0 %shard_map.102 = (bf16[512,2560]{1,0:T(8,128)(2,1)S(1)}, bf16[512,2560]{1,0:T(8,128)(2,1)S(1)}, bf16[512,2,512]{2,1,0:T(2,128)(2,1)S(1)}, bf16[8,2,1024]{2,1,0:T(2,128)(2,1)S(1)}) custom-call(s32[16]{0:T(128)S(1)} %copy-done.2, s32[1]{0:T(128)S(6)} %copy.11.owner_ref, s32[1]{0:T(128)S(6)} %copy.12.length_ref, bf16[8,2,1024]{2,1,0:T(2,128)(2,1)S(1)} %bitcast.9, ...), custom_call_target="tpu_custom_call" | custom-call | tf_op jit(solution)/shard_map/pallas_call | solution.py:493
  54.6 2.7 %shard_map.103 = (bf16[512,2560]{1,0:T(8,128)(2,1)}, bf16[512,2560]{1,0:T(8,128)(2,1)}, bf16[512,2,512]{2,1,0:T(2,128)(2,1)}, bf16[8,2,1024]{2,1,0:T(2,128)(2,1)}) custom-call(bf16[512,2560]{1,0:T(8,128)(2,1)S(1)} %get-tuple-element.12.refs_0_, bf16[512,2560]{1,0:T(8,128)(2,1)S(1)} %get-tuple-element.13.refs_1_, ...), custom_call_target="tpu_custom_call" | custom-call | tf_op jit(solution)/shard_map/pallas_call | solution.py:554
Async XLA Ops:
  1.9 1.2 %copy-start = (bf16[1,512,2,512]{3,2,1,0:T(2,128)(2,1)S(1)}, bf16[1,512,2,512]{3,2,1,0:T(2,128)(2,1)}, u32[]{:S(2)}) copy-start(bf16[1,512,2,512]{3,2,1,0:T(2,128)(2,1)} %param.8) | copy-start | bytes 3145732
  3.1 0.8 %copy-start.1 = (bf16[1,8,2,1024]{3,2,1,0:T(2,128)(2,1)S(1)}, bf16[1,8,2,1024]{3,2,1,0:T(2,128)(2,1)}, u32[]{:S(2)}) copy-start(bf16[1,8,2,1024]{3,2,1,0:T(2,128)(2,1)} %param.9) | copy-start | bytes 98308
  3.9 0.7 %copy-start.2 = (s32[16]{0:T(128)S(1)}, s32[16]{0:T(128)}, u32[]{:S(2)}) copy-start(s32[16]{0:T(128)} %order_ref.1) | copy-start | bytes 196

commit v4 on v3

--- a/solution.py
+++ b/solution.py
@@ -18,6 +18,8 @@
 TILES = RMAX // ROWS
 STACK = GROUP * ROWS
 STARTS = (0, 128, 384, 768)
+LOWS = (0, 128, 384, 0)
+LOW = 768
 WIDE = 1280
 SCALE = 1.0 / math.sqrt(HD)
 LOG2 = SCALE * math.log2(math.e)
@@ -188,6 +190,8 @@
     g_buf,
     k_own,
     v_own,
+    scores,
+    memo_o,
     raised,
     dprobs,
     stats,
@@ -244,27 +248,28 @@
         for i in range(TILES):
             seen = (i + 1) * ROWS
             base = STARTS[i]
-            raised[kv, base : base + seen] = dot_nt(k_own[:seen, lanes(kv)], stacked(q_buf, kv, i))
+            scores[LOWS[i] : LOWS[i] + seen] = dot_nt(k_own[:seen, lanes(kv)], stacked(q_buf, kv, i))
             dprobs[kv, base : base + seen] = dot_nt(v_own[:seen, lanes(kv)], stacked(g_buf, kv, i))
             for h in range(GROUP):
                 part = slice(h * ROWS, (h + 1) * ROWS)
                 blocks = [slice(base + c * ROWS, base + (c + 1) * ROWS) for c in range(i + 1)]
-                diagonal = jnp.where(tri, raised[kv, blocks[i], part], -1e30)
+                diagonal = jnp.where(tri, scores[LOWS[i] + i * ROWS : LOWS[i] + (i + 1) * ROWS, part], -1e30)
                 top = diagonal
                 for c in range(i):
-                    top = jnp.maximum(top, raised[kv, blocks[c], part])
+                    top = jnp.maximum(top, scores[LOWS[i] + c * ROWS : LOWS[i] + (c + 1) * ROWS, part])
                 top = jnp.max(top, axis=0, keepdims=True)
                 total = jnp.zeros((ROWS, ROWS), F32)
                 center = jnp.zeros((ROWS, ROWS), F32)
                 for c in range(i + 1):
-                    piece = diagonal if c == i else raised[kv, blocks[c], part]
+                    piece = diagonal if c == i else scores[LOWS[i] + c * ROWS : LOWS[i] + (c + 1) * ROWS, part]
                     piece = jnp.exp2((piece - top) * LOG2)
-                    raised[kv, blocks[c], part] = piece
+                    raised[kv, blocks[c], part] = piece.astype(BF16)
                     total = total + piece
                     center = center + piece * dprobs[kv, blocks[c], part]
                 stats[kv, i, 0:1, part] = top
                 stats[kv, i, 1:2, part] = jnp.sum(total, axis=0, keepdims=True)
                 stats[kv, i, 2:3, part] = jnp.sum(center, axis=0, keepdims=True)
+            memo_o[kv, i] = dot_tn(v_own[:seen, lanes(kv)], raised[kv, base : base + seen]).astype(BF16)
         return carry
 
     def prompt_part(kv, carry):
@@ -317,23 +322,22 @@
                 center = stats[kv, i, 4:5, part]
                 for c in range(i + 1):
                     at = slice(base + c * ROWS, base + (c + 1) * ROWS)
-                    probs = raised[kv, at, part] * factor
-                    low_p[at, part] = probs.astype(BF16)
-                    low_d[at, part] = (probs * ((dprobs[kv, at, part] - center) * SCALE)).astype(BF16)
-            own_p = low_p[base : base + seen]
-            own_d = low_d[base : base + seen]
+                    probs = raised[kv, at, part].astype(F32) * factor
+                    low = slice(LOWS[i] + c * ROWS, LOWS[i] + (c + 1) * ROWS)
+                    low_p[low, part] = probs.astype(BF16)
+                    low_d[low, part] = (probs * ((dprobs[kv, at, part] - center) * SCALE)).astype(BF16)
+            own_p = low_p[LOWS[i] : LOWS[i] + seen]
+            own_d = low_d[LOWS[i] : LOWS[i] + seen]
             sum_k[:seen] += dot_nn(own_d, query)
             sum_v[:seen] += dot_nn(own_p, grad)
-            result = dot_tn(
-                jnp.concatenate([front_p[kv, i], own_p], 0), jnp.concatenate([front_v, v_own[:seen, lanes(kv)]], 0)
-            )
+            result = memo_o[kv, i].astype(F32) * stats[kv, i, 3:4] + dot_tn(front_v, front_p[kv, i])
             grad_q = dot_tn(
-                jnp.concatenate([front_d[kv, i], own_d], 0), jnp.concatenate([front_k, k_own[:seen, lanes(kv)]], 0)
+                jnp.concatenate([front_k, k_own[:seen, lanes(kv)]], 0), jnp.concatenate([front_d[kv, i], own_d], 0)
             )
             for h in range(GROUP):
                 part = slice(h * ROWS, (h + 1) * ROWS)
-                out_ref[i * ROWS : (i + 1) * ROWS, head_lanes(kv, h)] = result[part].astype(BF16)
-                dq_ref[i * ROWS : (i + 1) * ROWS, head_lanes(kv, h)] = grad_q[part].astype(BF16)
+                out_ref[i * ROWS : (i + 1) * ROWS, head_lanes(kv, h)] = result[:, part].T.astype(BF16)
+                dq_ref[i * ROWS : (i + 1) * ROWS, head_lanes(kv, h)] = grad_q[:, part].T.astype(BF16)
         order = pairs()
         for c in range(TILES):
             at = slice(c * ROWS, (c + 1) * ROWS)
@@ -346,23 +350,31 @@
 
     cache[...] = cache_ref[...].reshape(cache.shape)
 
-    def first_copy(o):
-        return plane_copy(
+    def side(at_t, part):
+        return pl.ds(pl.multiple_of(at_t * width + part * half, half), half)
+
+    def first_copy(part):
+        return lambda o: plane_copy(
             grid,
             o,
-            lambda peer: cache.at[
-                :, pl.ds(pl.multiple_of(lax.rem(peer, grid.nt) * width, width), width)
-            ],
-            chunk(first, grid.c1),
-            send_1,
-            recv_1,
+            lambda peer: cache.at[:, side(lax.rem(peer, grid.nt), part)],
+            chunk(first.at[part], grid.c1),
+            send_1.at[part],
+            recv_1.at[part],
         )
 
     def mark_copy(o):
         return column_copy(grid, o, lambda peer: mark, chunk(marks, grid.c2), send_m, recv_m)
 
-    def second_copy(o):
-        return column_copy(grid, o, chunk(chosen, grid.c2), chunk(second, grid.c2), send_2, recv_2)
+    def second_copy(part):
+        return lambda o: column_copy(
+            grid,
+            o,
+            chunk(chosen.at[part], grid.c2),
+            chunk(second.at[part], grid.c2),
+            send_2.at[part],
+            recv_2.at[part],
+        )
 
     def third_copy(part):
         return lambda o: column_copy(
@@ -387,6 +399,16 @@
     in_plane = pl.ds(pl.multiple_of(u * grid.c1, grid.c1), grid.c1)
     in_column = pl.ds(pl.multiple_of(b * grid.c2, grid.c2), grid.c2)
 
+    def send_rows(part):
+        wait_recv_all(first_copy(part), grid.nu)
+        chosen[part] = dot_nn(pick[...], first[part]).astype(BF16)
+        start_all(second_copy(part), grid.nb)
+        second[part, in_column] = chosen[part, in_column]
+
+    def take_rows(part):
+        wait_recv_all(second_copy(part), grid.nb)
+        rows[:, part * half : (part + 1) * half] = dot_nn(shuffle(grid), second[part]).astype(BF16)
+
     def send_terms(part):
         outgoing[part] = dot_tn(shuffle(grid), terms[:, part * half : (part + 1) * half]).astype(BF16)
         start_all(third_copy(part), grid.nb)
@@ -419,9 +441,11 @@
         block = block + jnp.where(order_ref[i] == owner_ref[0], i, 0)
     mark[...] = jnp.full(mark.shape, block.astype(F32), F32)
     greet(grid)
-    start_all(first_copy, grid.nu)
+    start_all(first_copy(0), grid.nu)
     start_all(mark_copy, grid.nb)
-    first[in_plane] = cache[:, pl.ds(pl.multiple_of(t * width, width), width)]
+    start_all(first_copy(1), grid.nu)
+    for part in range(2):
+        first[part, in_plane] = cache[:, side(t, part)]
     marks[in_column] = mark[...]
     order = pairs()
     for j in range(TILES):
@@ -434,15 +458,14 @@
     pick[...] = choice(
         grid, jnp.concatenate([marks[...]] * many, 1) if many > 1 else marks[:, : grid.nu * grid.c1]
     )
-    wait_recv_all(first_copy, grid.nu)
-    chosen[...] = dot_nn(pick[...], first[...]).astype(BF16)
-    start_all(second_copy, grid.nb)
-    second[in_column] = chosen[in_column]
-    run(own_forward, 2, heads)
-    wait_recv_all(second_copy, grid.nb)
-    rows[...] = dot_nn(shuffle(grid), second[...]).astype(BF16)
+    send_rows(0)
+    run(own_forward, 2, 3)
+    send_rows(1)
+    run(own_forward, 3, heads)
+    take_rows(0)
     run(prompt_part, 0, heads // 2)
     send_terms(0)
+    take_rows(1)
     run(prompt_part, heads // 2, heads)
     send_terms(1)
     run(own_backward, 0, 1)
@@ -453,10 +476,10 @@
     finish(0)
     finish(1)
 
-    wait_send_all(first_copy, grid.nu)
     wait_send_all(mark_copy, grid.nb)
-    wait_send_all(second_copy, grid.nb)
     for part in range(2):
+        wait_send_all(first_copy(part), grid.nu)
+        wait_send_all(second_copy(part), grid.nb)
         wait_send_all(third_copy(part), grid.nb)
         wait_send_all(fourth_copy(part), grid.nu)
 
@@ -504,10 +527,10 @@
             pltpu.VMEM((grid.c1, grid.nt * width), BF16),
             pltpu.VMEM((grid.c2, HD), F32),
             pltpu.VMEM((all_rows, HD), F32),
-            pltpu.VMEM((all_blocks, width), BF16),
+            pltpu.VMEM((2, all_blocks, half), BF16),
             pltpu.VMEM((all_rows, all_blocks), BF16),
-            pltpu.VMEM((all_rows, width), BF16),
-            pltpu.VMEM((all_rows, width), BF16),
+            pltpu.VMEM((2, all_rows, half), BF16),
+            pltpu.VMEM((2, all_rows, half), BF16),
             pltpu.VMEM((all_rows, width), BF16),
             pltpu.VMEM((all_rows, width), BF16),
             pltpu.VMEM((2, all_rows, half), BF16),
@@ -518,22 +541,24 @@
             pltpu.VMEM(full, BF16),
             pltpu.VMEM((RMAX, width), BF16),
             pltpu.VMEM((RMAX, width), BF16),
-            pltpu.VMEM((heads, WIDE, STACK), F32),
+            pltpu.VMEM((LOW, STACK), F32),
+            pltpu.VMEM((heads, TILES, HD, STACK), BF16),
+            pltpu.VMEM((heads, WIDE, STACK), BF16),
             pltpu.VMEM((heads, WIDE, STACK), F32),
             pltpu.VMEM((heads, TILES, 8, STACK), F32),
             pltpu.VMEM((heads, TILES, PLEN, STACK), BF16),
             pltpu.VMEM((heads, TILES, PLEN, STACK), BF16),
-            pltpu.VMEM((WIDE, STACK), BF16),
-            pltpu.VMEM((WIDE, STACK), BF16),
+            pltpu.VMEM((LOW, STACK), BF16),
+            pltpu.VMEM((LOW, STACK), BF16),
             pltpu.VMEM((RMAX, HD), F32),
             pltpu.VMEM((RMAX, HD), F32),
             dma((2, heads)),
             dma((grid.nb,)),
             dma((grid.nb,)),
-            dma((grid.nu,)),
-            dma((grid.nu,)),
-            dma((grid.nb,)),
-            dma((grid.nb,)),
+            dma((2, grid.nu)),
+            dma((2, grid.nu)),
+            dma((2, grid.nb)),
+            dma((2, grid.nb)),
             dma((2, grid.nb)),
             dma((2, grid.nb)),
             dma((2, grid.nu)),

time: 57.7 us -> 55.6 us (0.964)
  Pallas kernels: 52.7 us -> 50.7 us
    pallas_call x1, Pallas kernels: 50 us -> 48 us  [local(): pl.pallas_call(functools.partial(kernel, grid), out_shape=(jax.ShapeDtype...]
where the time goes in v4:
time: 55.6 us; the launch traced here: 55.4 us
  Pallas kernels  50.7 us (91%)
  local copies, waits for them, and re-layouts  2.63 us (5%)
  between operations  2.1 us (4%)
    pallas_call x1, Pallas kernels, local(): pl.pallas_call(functools.partial(kernel, grid), out_shape=(jax.ShapeDtype...  48 us
    pallas_call x1, Pallas kernels, local(): pl.pallas_call(hand_on, out_shape=tuple((jax.ShapeDtypeStruct(x.shape, x....  2.73 us
    unnamed x6, local copies, waits for them, and re-layouts  2.63 us

profile of v4, /device:TPU:1, one launch (start us, length us, event | category | flops | bytes accessed | tf_op | source)
XLA Modules:
  0.0 55.4 jit_solution(6663069701711743645)
XLA Ops:
  1.9 0.0 copy-start
  1.9 1.2 %copy-done = bf16[1,512,2,512]{3,2,1,0:T(2,128)(2,1)S(1)} copy-done((bf16[1,512,2,512]{3,2,1,0:T(2,128)(2,1)S(1)}, bf16[1,512,2,512]{3,2,1,0:T(2,128)(2,1)}, u32[]{:S(2)}) %copy-start) | copy-done | bytes 1048600
  3.1 0.0 copy-start.1
  3.2 0.8 %copy-done.1 = bf16[1,8,2,1024]{3,2,1,0:T(2,128)(2,1)S(1)} copy-done((bf16[1,8,2,1024]{3,2,1,0:T(2,128)(2,1)S(1)}, bf16[1,8,2,1024]{3,2,1,0:T(2,128)(2,1)}, u32[]{:S(2)}) %copy-start.1) | copy-done | bytes 32792
  3.9 0.0 copy-start.2
  3.9 0.7 %copy-done.2 = s32[16]{0:T(128)S(1)} copy-done((s32[16]{0:T(128)S(1)}, s32[16]{0:T(128)}, u32[]{:S(2)}) %copy-start.2) | copy-done | bytes 88
  4.6 48.0 %shard_map.102 = (bf16[512,2560]{1,0:T(8,128)(2,1)S(1)}, bf16[512,2560]{1,0:T(8,128)(2,1)S(1)}, bf16[512,2,512]{2,1,0:T(2,128)(2,1)S(1)}, bf16[8,2,1024]{2,1,0:T(2,128)(2,1)S(1)}) custom-call(s32[16]{0:T(128)S(1)} %copy-done.2, s32[1]{0:T(128)S(6)} %copy.11.owner_ref, s32[1]{0:T(128)S(6)} %copy.12.length_ref, bf16[8,2,1024]{2,1,0:T(2,128)(2,1)S(1)} %bitcast.9, ...), custom_call_target="tpu_custom_call" | custom-call | tf_op jit(solution)/shard_map/pallas_call | solution.py:516
  52.5 2.7 %shard_map.103 = (bf16[512,2560]{1,0:T(8,128)(2,1)}, bf16[512,2560]{1,0:T(8,128)(2,1)}, bf16[512,2,512]{2,1,0:T(2,128)(2,1)}, bf16[8,2,1024]{2,1,0:T(2,128)(2,1)}) custom-call(bf16[512,2560]{1,0:T(8,128)(2,1)S(1)} %get-tuple-element.12.refs_0_, bf16[512,2560]{1,0:T(8,128)(2,1)S(1)} %get-tuple-element.13.refs_1_, ...), custom_call_target="tpu_custom_call" | custom-call | tf_op jit(solution)/shard_map/pallas_call | solution.py:579
Async XLA Ops:
  1.9 1.2 %copy-start = (bf16[1,512,2,512]{3,2,1,0:T(2,128)(2,1)S(1)}, bf16[1,512,2,512]{3,2,1,0:T(2,128)(2,1)}, u32[]{:S(2)}) copy-start(bf16[1,512,2,512]{3,2,1,0:T(2,128)(2,1)} %param.8) | copy-start | bytes 3145732
  3.1 0.8 %copy-start.1 = (bf16[1,8,2,1024]{3,2,1,0:T(2,128)(2,1)S(1)}, bf16[1,8,2,1024]{3,2,1,0:T(2,128)(2,1)}, u32[]{:S(2)}) copy-start(bf16[1,8,2,1024]{3,2,1,0:T(2,128)(2,1)} %param.9) | copy-start | bytes 98308
  3.9 0.7 %copy-start.2 = (s32[16]{0:T(128)S(1)}, s32[16]{0:T(128)}, u32[]{:S(2)}) copy-start(s32[16]{0:T(128)} %order_ref.1) | copy-start | bytes 196

commit v5 on v4

--- a/solution.py
+++ b/solution.py
@@ -173,6 +173,8 @@
     dq_ref,
     dkv_ref,
     cgrad_ref,
+    regroup,
+    pairing,
     cache,
     mark,
     marks,
@@ -338,7 +340,7 @@
                 part = slice(h * ROWS, (h + 1) * ROWS)
                 out_ref[i * ROWS : (i + 1) * ROWS, head_lanes(kv, h)] = result[:, part].T.astype(BF16)
                 dq_ref[i * ROWS : (i + 1) * ROWS, head_lanes(kv, h)] = grad_q[:, part].T.astype(BF16)
-        order = pairs()
+        order = pairing[...]
         for c in range(TILES):
             at = slice(c * ROWS, (c + 1) * ROWS)
             mixed = dot_tn(order, jnp.concatenate([sum_k[at].astype(BF16), sum_v[at].astype(BF16)], 0))
@@ -407,10 +409,10 @@
 
     def take_rows(part):
         wait_recv_all(second_copy(part), grid.nb)
-        rows[:, part * half : (part + 1) * half] = dot_nn(shuffle(grid), second[part]).astype(BF16)
+        rows[:, part * half : (part + 1) * half] = dot_nn(regroup[...], second[part]).astype(BF16)
 
     def send_terms(part):
-        outgoing[part] = dot_tn(shuffle(grid), terms[:, part * half : (part + 1) * half]).astype(BF16)
+        outgoing[part] = dot_tn(regroup[...], terms[:, part * half : (part + 1) * half]).astype(BF16)
         start_all(third_copy(part), grid.nb)
         third[part, in_column] = outgoing[part, in_column]
 
@@ -447,7 +449,9 @@
     for part in range(2):
         first[part, in_plane] = cache[:, side(t, part)]
     marks[in_column] = mark[...]
-    order = pairs()
+    regroup[...] = shuffle(grid)
+    pairing[...] = pairs()
+    order = pairing[...]
     for j in range(TILES):
         split = dot_nn(order, kv_ref[j * ROWS : (j + 1) * ROWS].reshape(2 * ROWS, width)).astype(BF16)
         k_own[j * ROWS : (j + 1) * ROWS] = split[:ROWS]
@@ -524,6 +528,8 @@
         in_specs=[smem] * 3 + [vmem] * 2 + [hbm] * 2,
         out_specs=(vmem,) * 4,
         scratch_shapes=[
+            pltpu.VMEM((all_rows, all_rows), BF16),
+            pltpu.VMEM((2 * ROWS, 2 * ROWS), BF16),
             pltpu.VMEM((grid.c1, grid.nt * width), BF16),
             pltpu.VMEM((grid.c2, HD), F32),
             pltpu.VMEM((all_rows, HD), F32),

time: 55.6 us -> 55.7 us (level)
  no operation moved by 1% of the time
where the time goes in v5:
time: 55.7 us; the launch traced here: 55.5 us
  Pallas kernels  50.8 us (91%)
  local copies, waits for them, and re-layouts  2.63 us (5%)
  between operations  2.1 us (4%)
    pallas_call x1, Pallas kernels, local(): pl.pallas_call(functools.partial(kernel, grid), out_shape=(jax.ShapeDtype...  48.1 us
    pallas_call x1, Pallas kernels, local(): pl.pallas_call(hand_on, out_shape=tuple((jax.ShapeDtypeStruct(x.shape, x....  2.73 us
    unnamed x6, local copies, waits for them, and re-layouts  2.63 us

profile of v5, /device:TPU:1, one launch (start us, length us, event | category | flops | bytes accessed | tf_op | source)
XLA Modules:
  0.0 55.5 jit_solution(10255931276825204184)
XLA Ops:
  1.9 0.0 copy-start
  1.9 1.2 %copy-done = bf16[1,512,2,512]{3,2,1,0:T(2,128)(2,1)S(1)} copy-done((bf16[1,512,2,512]{3,2,1,0:T(2,128)(2,1)S(1)}, bf16[1,512,2,512]{3,2,1,0:T(2,128)(2,1)}, u32[]{:S(2)}) %copy-start) | copy-done | bytes 1048600
  3.1 0.0 copy-start.1
  3.2 0.8 %copy-done.1 = bf16[1,8,2,1024]{3,2,1,0:T(2,128)(2,1)S(1)} copy-done((bf16[1,8,2,1024]{3,2,1,0:T(2,128)(2,1)S(1)}, bf16[1,8,2,1024]{3,2,1,0:T(2,128)(2,1)}, u32[]{:S(2)}) %copy-start.1) | copy-done | bytes 32792
  3.9 0.0 copy-start.2
  3.9 0.7 %copy-done.2 = s32[16]{0:T(128)S(1)} copy-done((s32[16]{0:T(128)S(1)}, s32[16]{0:T(128)}, u32[]{:S(2)}) %copy-start.2) | copy-done | bytes 88
  4.6 48.1 %shard_map.102 = (bf16[512,2560]{1,0:T(8,128)(2,1)S(1)}, bf16[512,2560]{1,0:T(8,128)(2,1)S(1)}, bf16[512,2,512]{2,1,0:T(2,128)(2,1)S(1)}, bf16[8,2,1024]{2,1,0:T(2,128)(2,1)S(1)}) custom-call(s32[16]{0:T(128)S(1)} %copy-done.2, s32[1]{0:T(128)S(6)} %copy.11.owner_ref, s32[1]{0:T(128)S(6)} %copy.12.length_ref, bf16[8,2,1024]{2,1,0:T(2,128)(2,1)S(1)} %bitcast.9, ...), custom_call_target="tpu_custom_call" | custom-call | tf_op jit(solution)/shard_map/pallas_call | solution.py:520
  52.6 2.7 %shard_map.103 = (bf16[512,2560]{1,0:T(8,128)(2,1)}, bf16[512,2560]{1,0:T(8,128)(2,1)}, bf16[512,2,512]{2,1,0:T(2,128)(2,1)}, bf16[8,2,1024]{2,1,0:T(2,128)(2,1)}) custom-call(bf16[512,2560]{1,0:T(8,128)(2,1)S(1)} %get-tuple-element.12.refs_0_, bf16[512,2560]{1,0:T(8,128)(2,1)S(1)} %get-tuple-element.13.refs_1_, ...), custom_call_target="tpu_custom_call" | custom-call | tf_op jit(solution)/shard_map/pallas_call | solution.py:585
Async XLA Ops:
  1.9 1.2 %copy-start = (bf16[1,512,2,512]{3,2,1,0:T(2,128)(2,1)S(1)}, bf16[1,512,2,512]{3,2,1,0:T(2,128)(2,1)}, u32[]{:S(2)}) copy-start(bf16[1,512,2,512]{3,2,1,0:T(2,128)(2,1)} %param.8) | copy-start | bytes 3145732
  3.1 0.8 %copy-start.1 = (bf16[1,8,2,1024]{3,2,1,0:T(2,128)(2,1)S(1)}, bf16[1,8,2,1024]{3,2,1,0:T(2,128)(2,1)}, u32[]{:S(2)}) copy-start(bf16[1,8,2,1024]{3,2,1,0:T(2,128)(2,1)} %param.9) | copy-start | bytes 98308
  3.9 0.7 %copy-start.2 = (s32[16]{0:T(128)S(1)}, s32[16]{0:T(128)}, u32[]{:S(2)}) copy-start(s32[16]{0:T(128)} %order_ref.1) | copy-start | bytes 196
